TPU v7x, 32 devices: a whole 2x2x4 slice. The times are simulated.
32 devices in a mesh: grp: 2 (over y), visit: 16 (over z, x, core).
Axes of the slice: x: 2, y: 2, z: 4, core: 2. Of those that a mesh axis runs over, the one named last changes fastest.
Arguments:
- science: float32 [8192, 1024], P(('grp', 'visit')), parts along dimension 0, may hold values from -6 to 6
- patches: float32 [256, 256, 256], P(('grp', 'visit')), parts along dimension 0, may hold values from -6 to 6
- margin: int32 [128, 3], P('grp'), parts along dimension 0, may hold values from 0 to 255, as said below
- kernel_coef: float32 [27, 128], P(None, ('grp', 'visit')), parts along dimension 1, may hold values from -4 to 4
- ccd_first: int32 [32], P('grp'), parts along dimension 0, may hold values 0 or 1
Outputs:
- patch_mean: float32 [256, 256, 256], P(('grp', 'visit')), parts along dimension 0
There are 2 independent parts, one for each index of `grp`. A program takes and returns all parts, laid end to end along the dimension named above; each array names one. Nothing has to cross between parts.
Inputs may be any that keep to these rules, and one draw needn't show every extreme that they name: `margin`: column 0 is a patch id, columns 1 and 2 are offsets below 256. A tile of strip d names a patch owned by strip d - 1, d or d + 1. Among the 4 tiles of one strip at most 2 name patches of one owner (patch id // 8), and in every strip some owner is named exactly 2 times.
All inputs are finite; a program needn't handle non-finite values.
Results may differ from a plain program's by a relative error of at most 0.004.
Values may be sent and summed in bfloat16 or wider, within the bound.
A program may use at most 64 MiB of HBM per device.

v0:
```python
import functools
import math

import jax
import jax.numpy as jnp
from jax import lax
from jax.experimental import pallas as pl
from jax.experimental.pallas import tpu as pltpu
from jax.sharding import PartitionSpec as P

RADIUS = 10
SIGMAS = 3
ORDERS = 3
PAIRS = SIGMAS * ORDERS
EDGE = 16
SIDE = 128
BF = jnp.bfloat16
F32 = jnp.float32


def sigma_of(g):
    return 0.75 * 2.0**g


def norm_of(g):
    sigma = sigma_of(g)
    return sum(math.exp(-u * u / (2.0 * sigma * sigma)) for u in range(-RADIUS, RADIUS + 1))


def basis_functions(u, g):
    sigma = sigma_of(g)
    inside = jnp.abs(u) <= RADIUS
    base = jnp.where(inside, jnp.exp(u * u * (-1.0 / (2.0 * sigma * sigma))) * (1.0 / norm_of(g)), 0.0)
    scaled = u * (1.0 / sigma)
    first = base * scaled
    return base, first, first * scaled


def named_tiles(margin, strip, owner, owners, per, owned, slots):
    valid = (strip >= 0) & (strip < owners)
    row = jnp.clip(strip, 0, owners - 1) * per
    tiles = [jnp.int32(0)] * slots
    locals_ = [jnp.int32(0)] * slots
    there = [jnp.int32(0)] * slots
    count = jnp.int32(0)
    for t in range(per):
        patch = margin[row + t, 0]
        who = lax.div(patch, jnp.int32(owned))
        named = ((who == owner) & valid).astype(jnp.int32)
        for k in range(slots):
            hit = (named == 1) & (count == k)
            tiles[k] = jnp.where(hit, jnp.int32(t), tiles[k])
            locals_[k] = jnp.where(hit, patch - who * owned, locals_[k])
            there[k] = jnp.where(hit, jnp.int32(1), there[k])
        count = count + named
    return tiles, locals_, there


def one_hot(size, shift):
    rows = lax.broadcasted_iota(jnp.int32, (size, size), 0)
    cols = lax.broadcasted_iota(jnp.int32, (size, size), 1)
    return jnp.where(((rows - cols + shift) & (size - 1)) == 0, 1.0, 0.0).astype(BF)


def moved(x, down, right):
    size = x.shape[0]
    a = jnp.dot(one_hot(size, -down), x, preferred_element_type=F32).astype(BF)
    return jnp.dot(a, one_hot(size, right), preferred_element_type=F32).astype(BF)


def match_kernel(
    owners, per, owned, tile, slots,
    margin, coef, ccd, patches_h, science_h,
    out_h,
    patches, science, stage, pool, ext, halo, tab, mixed, mixed_small, across, v_mid, v_out, diff, back,
    load_sem, tile_send, tile_recv, halo_send, halo_recv, back_send, back_recv, own_sem,
):
    d = lax.axis_index("visit")
    has_low, has_high = d > 0, d < owners - 1
    low, high = d - 1, d + 1
    half, quarter = tile // 2, tile // 4
    mid_depth, small_depth = half + 2 * EDGE, quarter + 2 * EDGE
    width = tile + 2 * SIDE
    strip = per * tile

    patch_load = pltpu.make_async_copy(patches_h, patches, load_sem.at[0])
    science_load = pltpu.make_async_copy(science_h, science, load_sem.at[1])
    patch_load.start()
    science_load.start()

    barrier = pltpu.get_barrier_semaphore()

    @pl.when(has_low)
    def _():
        pl.semaphore_signal(barrier, inc=1, device_id={"visit": low}, device_id_type=pl.DeviceIdType.MESH)

    @pl.when(has_high)
    def _():
        pl.semaphore_signal(barrier, inc=1, device_id={"visit": high}, device_id_type=pl.DeviceIdType.MESH)

    ext[:, pl.ds(0, SIDE)] = jnp.zeros((tile + 2 * EDGE, SIDE), BF)
    ext[:, pl.ds(SIDE + strip, SIDE)] = jnp.zeros((tile + 2 * EDGE, SIDE), BF)
    _, high_local, _ = named_tiles(margin, high, d, owners, per, owned, slots)
    _, low_local, _ = named_tiles(margin, low, d, owners, per, owned, slots)
    _, own_local, _ = named_tiles(margin, d, d, owners, per, owned, slots)
    patch_load.wait()

    def remote(src, dst, send, recv, target):
        return pltpu.make_async_remote_copy(
            src_ref=src, dst_ref=dst, send_sem=send, recv_sem=recv,
            device_id={"visit": target}, device_id_type=pl.DeviceIdType.MESH,
        )

    def tile_to_high(k, target):
        return remote(stage.at[k], pool.at[k], tile_send.at[k], tile_recv.at[k], target)

    def tile_to_low(k, target):
        j = slots + k
        return remote(stage.at[j], pool.at[2 * slots + k], tile_send.at[j], tile_recv.at[j], target)

    for k in range(slots):
        stage[k] = patches[high_local[k]].astype(BF)
        stage[slots + k] = patches[low_local[k]].astype(BF)
    pl.semaphore_wait(barrier, has_low.astype(jnp.int32) + has_high.astype(jnp.int32))
    for k in range(slots):

        @pl.when(has_high)
        def _():
            tile_to_high(k, high).start()

        @pl.when(has_low)
        def _():
            tile_to_low(k, low).start()

    for k in range(slots):
        pool[slots + k] = patches[own_local[k]].astype(BF)

    rows = lax.broadcasted_iota(jnp.int32, (half, mid_depth), 0)
    cols = lax.broadcasted_iota(jnp.int32, (half, mid_depth), 1)
    u = (cols - rows - EDGE).astype(F32)
    for g in range(SIGMAS):
        for v, table in enumerate(basis_functions(u, g)):
            tab[g * ORDERS + v] = table

    def mix_tile(t, carry):
        for g in range(SIGMAS):
            for h in range(ORDERS):
                p = g * ORDERS + h
                total = coef[p * ORDERS, t] * tab[g * ORDERS]
                for v in range(1, ORDERS):
                    total = total + coef[p * ORDERS + v, t] * tab[g * ORDERS + v]
                total = total.astype(BF)
                mixed[t, pl.ds(p * half, half), :] = total
                mixed_small[t, pl.ds(p * quarter, quarter), :] = total[:quarter, :small_depth]
        return carry

    lax.fori_loop(0, per, mix_tile, 0)

    def across_rows(b, carry):
        r = lax.broadcasted_iota(jnp.int32, (SIDE, tile), 0) + b * SIDE
        c = lax.broadcasted_iota(jnp.int32, (SIDE, tile), 1)
        w = (r - c - SIDE).astype(F32)
        for g in range(SIGMAS):
            for h, table in enumerate(basis_functions(w, g)):
                start = pl.multiple_of((g * ORDERS + h) * width + b * SIDE, SIDE)
                across[pl.ds(start, SIDE), :] = table.astype(BF)
        return carry

    lax.fori_loop(0, width // SIDE, across_rows, 0)

    who = [lax.div(margin[d * per + t, 0], jnp.int32(owned)) for t in range(per)]
    places = []
    for t in range(per):
        rank = jnp.int32(0)
        for s in range(t):
            rank = rank + (who[s] == who[t]).astype(jnp.int32)
        places.append(jnp.clip((who[t] - d + 1) * slots + rank, 0, 3 * slots - 1))

    @pl.when(has_low)
    def _():
        for k in range(slots):
            tile_to_high(k, low).wait_recv()

    @pl.when(has_high)
    def _():
        for k in range(slots):
            tile_to_low(k, high).wait_recv()

    def align(t, carry):
        place = places[0]
        for s in range(1, per):
            place = jnp.where(t == s, places[s], place)
        shifted = moved(pool[place], margin[d * per + t, 1], margin[d * per + t, 2])
        ext[pl.ds(EDGE, tile), pl.ds(pl.multiple_of(SIDE + t * tile, SIDE), tile)] = shifted
        return carry

    lax.fori_loop(0, per, align, 0)

    def halo_to_high(target):
        return remote(
            ext.at[pl.ds(tile, EDGE), pl.ds(SIDE, strip)], halo.at[0], halo_send.at[0], halo_recv.at[0], target
        )

    def halo_to_low(target):
        return remote(
            ext.at[pl.ds(EDGE, EDGE), pl.ds(SIDE, strip)], halo.at[1], halo_send.at[1], halo_recv.at[1], target
        )

    @pl.when(has_high)
    def _():
        halo_to_high(high).start()

    @pl.when(has_low)
    def _():
        halo_to_low(low).start()

    def window(first, depth, t):
        return ext[pl.ds(first, depth), pl.ds(pl.multiple_of(t * tile, SIDE), width)]

    def vertical_mid(t, carry):
        result = jnp.dot(mixed[t], window(quarter, mid_depth, t), preferred_element_type=F32).astype(BF)
        for p in range(PAIRS):
            v_mid[pl.ds(pl.multiple_of(t * half, half), half), pl.ds(p * width, width)] = result[p * half : (p + 1) * half]
        return carry

    lax.fori_loop(0, per, vertical_mid, 0)
    science_load.wait()

    def across_mid(t, carry):
        start = pl.multiple_of(t * half, half)
        matched = jnp.dot(v_mid[pl.ds(start, 2 * half), :], across[...], preferred_element_type=F32)
        for i in range(2):
            sky = science[pl.ds(quarter, half), pl.ds(pl.multiple_of((t + i) * tile, SIDE), tile)]
            diff[t + i, pl.ds(quarter, half), :] = (sky - matched[i * half : (i + 1) * half]).astype(BF)
        return carry

    lax.fori_loop(0, per // 2, lambda i, c: across_mid(2 * i, c), 0)

    @pl.when(has_low)
    def _():
        halo_to_high(low).wait_recv()

    @pl.when(has_high)
    def _():
        halo_to_low(high).wait_recv()

    keep_top = has_low & (ccd[d] == 0)
    keep_bottom = has_high & (ccd[jnp.minimum(d + 1, owners - 1)] == 0)
    nothing = jnp.zeros((EDGE, strip), BF)
    ext[pl.ds(0, EDGE), pl.ds(SIDE, strip)] = jnp.where(keep_top, halo[0], nothing)
    ext[pl.ds(EDGE + tile, EDGE), pl.ds(SIDE, strip)] = jnp.where(keep_bottom, halo[1], nothing)

    def vertical_out(t, carry):
        for i, first in enumerate((0, tile - quarter)):
            result = jnp.dot(mixed_small[t], window(first, small_depth, t), preferred_element_type=F32).astype(BF)
            start = pl.multiple_of(t * half + i * quarter, quarter)
            for p in range(PAIRS):
                v_out[pl.ds(start, quarter), pl.ds(p * width, width)] = result[p * quarter : (p + 1) * quarter]
        return carry

    lax.fori_loop(0, per, vertical_out, 0)

    def across_out(t, carry):
        start = pl.multiple_of(t * half, half)
        matched = jnp.dot(v_out[pl.ds(start, 2 * half), :], across[...], preferred_element_type=F32)
        for i in range(4):
            first = (i % 2) * (tile - quarter)
            s = t + i // 2
            sky = science[pl.ds(first, quarter), pl.ds(pl.multiple_of(s * tile, SIDE), tile)]
            diff[s, pl.ds(first, quarter), :] = (sky - matched[i * quarter : (i + 1) * quarter]).astype(BF)
        return carry

    lax.fori_loop(0, per // 2, lambda i, c: across_out(2 * i, c), 0)

    to_low, _, _ = named_tiles(margin, d, low, owners, per, owned, slots)
    to_high, _, _ = named_tiles(margin, d, high, owners, per, owned, slots)
    to_own, _, _ = named_tiles(margin, d, d, owners, per, owned, slots)

    def returned(t):
        return moved(diff[t], -margin[d * per + t, 1], -margin[d * per + t, 2])

    def back_to_low(k, target):
        return remote(back.at[k], out_h.at[2 * slots + k], back_send.at[k], back_recv.at[k], target)

    def back_to_high(k, target):
        j = 2 * slots + k
        return remote(back.at[j], out_h.at[k], back_send.at[slots + k], back_recv.at[slots + k], target)

    def own_copy(k):
        return pltpu.make_async_copy(back.at[slots + k], out_h.at[slots + k], own_sem.at[k])

    for k in range(slots):
        back[k] = returned(to_low[k])

        @pl.when(has_low)
        def _():
            back_to_low(k, low).start()

        back[2 * slots + k] = returned(to_high[k])

        @pl.when(has_high)
        def _():
            back_to_high(k, high).start()

    for k in range(slots):
        back[slots + k] = returned(to_own[k])
        own_copy(k).start()
    for k in range(slots):
        own_copy(k).wait()

    @pl.when(has_low)
    def _():
        for k in range(slots):
            tile_to_low(k, low).wait_send()
            back_to_low(k, low).wait_send()
        halo_to_low(low).wait_send()
        for k in range(slots):
            back_to_high(k, low).wait_recv()

    @pl.when(has_high)
    def _():
        for k in range(slots):
            tile_to_high(k, high).wait_send()
            back_to_high(k, high).wait_send()
        halo_to_high(high).wait_send()
        for k in range(slots):
            back_to_low(k, high).wait_recv()


def mean_kernel(owners, per, owned, slots, margin, arrived, out_h, sums, sems):
    d = lax.axis_index("visit")
    ids, there = [], []
    for strip in (d - 1, d, d + 1):
        _, local, present = named_tiles(margin, strip, d, owners, per, owned, slots)
        ids += local
        there += present

    def copy(p):
        return pltpu.make_async_copy(sums.at[p], out_h.at[p], sems.at[p])

    def patch(p, carry):
        hits = [((ids[j] == p) & (there[j] == 1)) for j in range(3 * slots)]
        count = sum(hit.astype(jnp.int32) for hit in hits)
        scale = 1.0 / jnp.maximum(jnp.full((1, 1), count, jnp.int32).astype(F32), 1.0)
        sums[p] = jnp.zeros(sums.shape[1:], F32)
        for j, hit in enumerate(hits):

            @pl.when(hit)
            def _():
                sums[p] += arrived[j].astype(F32) * scale

        copy(p).start()
        return carry

    lax.fori_loop(0, owned, patch, 0)

    def finish(p, carry):
        copy(p).wait()
        return carry

    lax.fori_loop(0, owned, finish, 0)


def body(science, patches, margin, kernel_coef, ccd_first):
    owners = lax.axis_size("visit")
    owned, tile = patches.shape[0], patches.shape[1]
    per = science.shape[1] // tile
    slots = per // 2
    half, quarter = tile // 2, tile // 4
    width = tile + 2 * SIDE
    strip = per * tile
    smem = pl.BlockSpec(memory_space=pltpu.SMEM)
    anywhere = pl.BlockSpec(memory_space=pl.ANY)
    dma = pltpu.SemaphoreType.DMA
    arrived = pl.pallas_call(
        functools.partial(match_kernel, owners, per, owned, tile, slots),
        out_shape=jax.ShapeDtypeStruct((3 * slots, tile, tile), BF),
        in_specs=[smem, smem, smem, anywhere, anywhere],
        out_specs=anywhere,
        scratch_shapes=[
            pltpu.VMEM((owned, tile, tile), F32),
            pltpu.VMEM((tile, strip), F32),
            pltpu.VMEM((2 * slots, tile, tile), BF),
            pltpu.VMEM((3 * slots, tile, tile), BF),
            pltpu.VMEM((tile + 2 * EDGE, strip + 2 * SIDE), BF),
            pltpu.VMEM((2, EDGE, strip), BF),
            pltpu.VMEM((PAIRS, half, half + 2 * EDGE), F32),
            pltpu.VMEM((per, PAIRS * half, half + 2 * EDGE), BF),
            pltpu.VMEM((per, PAIRS * quarter, quarter + 2 * EDGE), BF),
            pltpu.VMEM((PAIRS * width, tile), BF),
            pltpu.VMEM((per * half, PAIRS * width), BF),
            pltpu.VMEM((per * half, PAIRS * width), BF),
            pltpu.VMEM((per, tile, tile), BF),
            pltpu.VMEM((3 * slots, tile, tile), BF),
            dma((2,)),
            dma((2 * slots,)),
            dma((2 * slots,)),
            dma((2,)),
            dma((2,)),
            dma((2 * slots,)),
            dma((2 * slots,)),
            dma((slots,)),
        ],
        compiler_params=pltpu.CompilerParams(
            collective_id=0, has_side_effects=True, vmem_limit_bytes=48 * 1024 * 1024
        ),
        name="match",
    )(margin, kernel_coef, ccd_first, patches, science)
    return pl.pallas_call(
        functools.partial(mean_kernel, owners, per, owned, slots),
        out_shape=jax.ShapeDtypeStruct(patches.shape, F32),
        in_specs=[smem, pl.BlockSpec(memory_space=pltpu.VMEM)],
        out_specs=anywhere,
        scratch_shapes=[pltpu.VMEM(patches.shape, F32), dma((owned,))],
        compiler_params=pltpu.CompilerParams(vmem_limit_bytes=16 * 1024 * 1024),
        name="mean",
    )(margin, arrived)


def solution(mesh):
    in_specs = (
        P(("grp", "visit"), None),
        P(("grp", "visit"), None, None),
        P("grp", None),
        P(None, ("grp", "visit")),
        P("grp"),
    )
    out_specs = P(("grp", "visit"), None, None)
    return jax.shard_map(body, mesh=mesh, in_specs=in_specs, out_specs=out_specs, check_vma=False)
```

profile of v0, /device:TPU:1, one launch (start us, length us, event | category | flops | bytes accessed | tf_op | source)
XLA Modules:
  0.0 33.6 jit_solution(16476408936248170822)
XLA Ops:
  0.0 0.8 %copy.7.coef = f32[27,4]{1,0:T(8,128)S(1)} copy(f32[27,4]{0,1:T(4,128)} %param.8) | data formatting | bytes 864 | tf_op args[3]
  0.8 0.8 %copy.8.margin = s32[64,3]{1,0:T(8,128)S(1)} copy(s32[64,3]{0,1:T(4,128)} %param.7) | data formatting | bytes 1536 | tf_op args[2]
  1.5 0.0 copy-start
  1.5 1.6 %copy-done = f32[8,256,256]{2,1,0:T(8,128)S(1)} copy-done((f32[8,256,256]{2,1,0:T(8,128)S(1)}, f32[8,256,256]{2,1,0:T(8,128)}, u32[]{:S(2)}) %copy-start) | copy-done | bytes 2097176
  3.1 0.0 copy-start.1
  3.1 1.2 %copy-done.1 = f32[256,1024]{1,0:T(8,128)S(1)} copy-done((f32[256,1024]{1,0:T(8,128)S(1)}, f32[256,1024]{1,0:T(8,128)}, u32[]{:S(2)}) %copy-start.1) | copy-done | bytes 1048600
  4.4 0.0 copy-start.2
  4.4 0.7 %copy-done.2 = s32[16]{0:T(128)S(1)} copy-done((s32[16]{0:T(128)S(1)}, s32[16]{0:T(128)}, u32[]{:S(2)}) %copy-start.2) | copy-done | bytes 88
  5.0 25.9 %match.1.arrived = bf16[6,256,256]{2,1,0:T(8,128)(2,1)S(1)} custom-call(s32[64,3]{1,0:T(8,128)S(1)} %copy.8.margin, f32[27,4]{1,0:T(8,128)S(1)} %copy.7.coef, s32[16]{0:T(128)S(1)} %copy-done.2, f32[8,256,256]{2,1,0:T(8,128)S(1)} %copy-done, f32[256,1024]{1,0:T(8,128)S(1)} %copy-done.1), custom_call_target="tpu_custom_call" | custom-call | tf_op jit(solution)/shard_map/match/pallas_call | solution.py:375
  31.0 2.6 %mean.1 = f32[8,256,256]{2,1,0:T(8,128)} custom-call(s32[64,3]{1,0:T(8,128)S(1)} %copy.8.margin, bf16[6,256,256]{2,1,0:T(8,128)(2,1)S(1)} %match.1.arrived), custom_call_target="tpu_custom_call" | custom-call | tf_op jit(solution)/shard_map/mean/pallas_call | solution.py:409
Async XLA Ops:
  1.5 1.6 %copy-start = (f32[8,256,256]{2,1,0:T(8,128)S(1)}, f32[8,256,256]{2,1,0:T(8,128)}, u32[]{:S(2)}) copy-start(f32[8,256,256]{2,1,0:T(8,128)} %patches_h.1) | copy-start | bytes 6291460
  3.1 1.2 %copy-start.1 = (f32[256,1024]{1,0:T(8,128)S(1)}, f32[256,1024]{1,0:T(8,128)}, u32[]{:S(2)}) copy-start(f32[256,1024]{1,0:T(8,128)} %science_h.1) | copy-start | bytes 3145732
  4.4 0.7 %copy-start.2 = (s32[16]{0:T(128)S(1)}, s32[16]{0:T(128)}, u32[]{:S(2)}) copy-start(s32[16]{0:T(128)} %ccd.1) | copy-start | bytes 196
where the time goes:
time: 33.8 us; the launch traced here: 33.6 us
  Pallas kernels  28.5 us (84%)
  local copies, waits for them, and re-layouts  5.01 us (15%)
    pallas_call x1, Pallas kernels, body(): pl.pallas_call(functools.partial(match_kernel, owners, per, owned, tile,...  25.9 us
    unnamed x8, local copies, waits for them, and re-layouts  5.01 us
    pallas_call x1, Pallas kernels, body(): pl.pallas_call(functools.partial(mean_kernel, owners, per, owned, slots),...  2.61 us

commit v1 on v0

v1 whole, which is shorter than its diff:
```python
import functools
import math

import jax
import jax.numpy as jnp
from jax import lax
from jax.experimental import pallas as pl
from jax.experimental.pallas import tpu as pltpu
from jax.sharding import PartitionSpec as P

RADIUS = 10
SIGMAS = 3
ORDERS = 3
PAIRS = SIGMAS * ORDERS
EDGE = 16
SIDE = 128
BF = jnp.bfloat16
F32 = jnp.float32


def sigma_of(g):
    return 0.75 * 2.0**g


def norm_of(g):
    sigma = sigma_of(g)
    return sum(math.exp(-u * u / (2.0 * sigma * sigma)) for u in range(-RADIUS, RADIUS + 1))


def basis_functions(u, g):
    sigma = sigma_of(g)
    inside = jnp.abs(u) <= RADIUS
    base = jnp.where(inside, jnp.exp(u * u * (-1.0 / (2.0 * sigma * sigma))) * (1.0 / norm_of(g)), 0.0)
    scaled = u * (1.0 / sigma)
    first = base * scaled
    return base, first, first * scaled


def named_tiles(margin, strip, owner, owners, per, owned, slots):
    valid = (strip >= 0) & (strip < owners)
    row = (jnp.clip(strip, 0, owners - 1) * per).astype(jnp.int32)
    tiles = [row] * slots
    locals_ = [jnp.int32(0)] * slots
    there = [jnp.int32(0)] * slots
    count = jnp.int32(0)
    for t in range(per):
        patch = margin[0, row + t]
        who = lax.div(patch, jnp.int32(owned))
        named = ((who == owner) & valid).astype(jnp.int32)
        for k in range(slots):
            hit = (named == 1) & (count == k)
            tiles[k] = jnp.where(hit, row + t, tiles[k])
            locals_[k] = jnp.where(hit, patch - who * owned, locals_[k])
            there[k] = jnp.where(hit, jnp.int32(1), there[k])
        count = count + named
    return tiles, locals_, there


def one_hot(size, shift):
    rows = lax.broadcasted_iota(jnp.int32, (size, size), 0)
    cols = lax.broadcasted_iota(jnp.int32, (size, size), 1)
    return jnp.where(((rows - cols + shift) & (size - 1)) == 0, 1.0, 0.0).astype(BF)


def moved(down, x, right):
    a = jnp.dot(down, x, preferred_element_type=F32).astype(BF)
    return jnp.dot(a, right, preferred_element_type=F32).astype(BF)


def match_kernel(
    owners, per, owned, tile, slots,
    margin, coef, ccd, patches_h, science_h,
    out_h,
    patches, science, stage, pool, forth, ext, halo, tab, mixed, across, column, diff, parcel, landed, back,
    load_sem, tile_send, tile_recv, halo_send, halo_recv, back_send, back_recv, out_sem,
):
    d = lax.axis_index("visit")
    has_low, has_high = d > 0, d < owners - 1
    low, high = d - 1, d + 1
    chunks = 4
    chunk = tile // chunks
    depth = chunk + 2 * EDGE
    width = tile + SIDE
    places = 3 * slots

    barrier = pltpu.get_barrier_semaphore()

    @pl.when(has_low)
    def _():
        pl.semaphore_signal(barrier, inc=1, device_id={"visit": low}, device_id_type=pl.DeviceIdType.MESH)

    @pl.when(has_high)
    def _():
        pl.semaphore_signal(barrier, inc=1, device_id={"visit": high}, device_id_type=pl.DeviceIdType.MESH)

    patch_load = pltpu.make_async_copy(patches_h, patches, load_sem.at[0])
    science_load = pltpu.make_async_copy(science_h, science, load_sem.at[1])
    patch_load.start()
    science_load.start()

    high_tiles, high_local, _ = named_tiles(margin, high, d, owners, per, owned, slots)
    low_tiles, low_local, _ = named_tiles(margin, low, d, owners, per, owned, slots)
    own_tiles, own_local, _ = named_tiles(margin, d, d, owners, per, owned, slots)
    from_low, _, _ = named_tiles(margin, d, low, owners, per, owned, slots)
    from_high, _, _ = named_tiles(margin, d, high, owners, per, owned, slots)
    arriving = from_low + own_tiles + from_high
    returning = low_tiles + own_tiles + high_tiles

    def remote(src, dst, send, recv, target):
        return pltpu.make_async_remote_copy(
            src_ref=src, dst_ref=dst, send_sem=send, recv_sem=recv,
            device_id={"visit": target}, device_id_type=pl.DeviceIdType.MESH,
        )

    def tile_to_high(k, target):
        return remote(stage.at[k], pool.at[k], tile_send.at[k], tile_recv.at[k], target)

    def tile_to_low(k, target):
        j = slots + k
        return remote(stage.at[j], pool.at[2 * slots + k], tile_send.at[j], tile_recv.at[j], target)

    patch_load.wait()
    for k in range(slots):
        stage[k] = patches[high_local[k]].astype(BF)
        stage[slots + k] = patches[low_local[k]].astype(BF)
    pl.semaphore_wait(barrier, has_low.astype(jnp.int32) + has_high.astype(jnp.int32))
    for k in range(slots):

        @pl.when(has_high)
        def _():
            tile_to_high(k, high).start()

        @pl.when(has_low)
        def _():
            tile_to_low(k, low).start()

    for k in range(slots):
        pool[slots + k] = patches[own_local[k]].astype(BF)

    def align(j):
        t = arriving[j]
        forth[j] = moved(one_hot(tile, -margin[1, t]), pool[j], one_hot(tile, margin[2, t]))

    rows = lax.broadcasted_iota(jnp.int32, (chunk, depth), 0)
    cols = lax.broadcasted_iota(jnp.int32, (chunk, depth), 1)
    u = (cols - rows - EDGE).astype(F32)
    for g in range(SIGMAS):
        for v, table in enumerate(basis_functions(u, g)):
            tab[g * ORDERS + v] = table

    def mix_tile(t, carry):
        for g in range(SIGMAS):
            for h in range(ORDERS):
                p = g * ORDERS + h
                total = coef[t, p * ORDERS] * tab[g * ORDERS]
                for v in range(1, ORDERS):
                    total = total + coef[t, p * ORDERS + v] * tab[g * ORDERS + v]
                mixed[t, pl.ds(p * chunk, chunk), :] = total.astype(BF)
        return carry

    lax.fori_loop(0, per, mix_tile, 0)

    def across_rows(b, carry):
        r = lax.broadcasted_iota(jnp.int32, (SIDE, tile), 0)
        c = lax.broadcasted_iota(jnp.int32, (SIDE, tile), 1)
        side = jnp.where(r < SIDE // 2, r + tile, r - SIDE)
        w = (jnp.where(b * SIDE < tile, r + b * SIDE, side) - c).astype(F32)
        for g in range(SIGMAS):
            for h, table in enumerate(basis_functions(w, g)):
                start = pl.multiple_of((g * ORDERS + h) * width + b * SIDE, SIDE)
                across[pl.ds(start, SIDE), :] = table.astype(BF)
        return carry

    lax.fori_loop(0, width // SIDE, across_rows, 0)

    for k in range(slots):
        align(slots + k)

    who = [lax.div(margin[0, d * per + t], jnp.int32(owned)) for t in range(per)]
    place = []
    for t in range(per):
        rank = jnp.int32(0)
        for s in range(t):
            rank = rank + (who[s] == who[t]).astype(jnp.int32)
        place.append(jnp.clip((who[t] - d + 1) * slots + rank, 0, places - 1))

    for k in range(slots):

        @pl.when(has_low)
        def _():
            tile_to_high(k, low).wait_recv()
            align(k)

        @pl.when(has_high)
        def _():
            tile_to_low(k, high).wait_recv()
            align(2 * slots + k)

    for t in range(per):
        ext[t, pl.ds(EDGE, tile), pl.ds(0, tile)] = forth[place[t]]

    def halo_to_high(target):
        return remote(
            ext.at[:, pl.ds(tile, EDGE), pl.ds(0, tile)], halo.at[0], halo_send.at[0], halo_recv.at[0], target
        )

    def halo_to_low(target):
        return remote(
            ext.at[:, pl.ds(EDGE, EDGE), pl.ds(0, tile)], halo.at[1], halo_send.at[1], halo_recv.at[1], target
        )

    @pl.when(has_high)
    def _():
        halo_to_high(high).start()

    @pl.when(has_low)
    def _():
        halo_to_low(low).start()

    def fill_sides(first, count):
        lane = lax.broadcasted_iota(jnp.int32, (count, SIDE), 1)
        none = jnp.zeros((count, SIDE), F32)
        for t in range(per):
            right = ext[t + 1, pl.ds(first, count), pl.ds(0, SIDE)].astype(F32) if t + 1 < per else none
            left = ext[t - 1, pl.ds(first, count), pl.ds(tile - SIDE, SIDE)].astype(F32) if t > 0 else none
            ext[t, pl.ds(first, count), pl.ds(tile, SIDE)] = jnp.where(lane < SIDE // 2, right, left).astype(BF)

    fill_sides(EDGE, tile)
    science_load.wait()

    def chunk_to_low(k, c, target):
        at = pl.ds(pl.multiple_of(c * chunk, chunk), chunk)
        return remote(
            parcel.at[k, at], landed.at[slots + k, at], back_send.at[c, k], back_recv.at[c, k], target
        )

    def chunk_to_high(k, c, target):
        j = slots + k
        at = pl.ds(pl.multiple_of(c * chunk, chunk), chunk)
        return remote(parcel.at[j, at], landed.at[k, at], back_send.at[c, j], back_recv.at[c, j], target)

    def one_chunk(i, carry):
        c = lax.rem(i + 1, chunks)
        at = pl.ds(pl.multiple_of(c * chunk, chunk), chunk)

        @pl.when(i == chunks - 2)
        def _():
            @pl.when(has_low)
            def _():
                halo_to_high(low).wait_recv()

            @pl.when(has_high)
            def _():
                halo_to_low(high).wait_recv()

            keep_top = has_low & (ccd[d] == 0)
            keep_bottom = has_high & (ccd[jnp.minimum(d + 1, owners - 1)] == 0)
            nothing = jnp.zeros((EDGE, tile), BF)
            for t in range(per):
                ext[t, pl.ds(0, EDGE), pl.ds(0, tile)] = jnp.where(keep_top, halo[0, t], nothing)
                ext[t, pl.ds(EDGE + tile, EDGE), pl.ds(0, tile)] = jnp.where(keep_bottom, halo[1, t], nothing)
            fill_sides(0, EDGE)
            fill_sides(EDGE + tile, EDGE)

        window = pl.ds(pl.multiple_of(c * chunk, chunk), depth)
        for t in range(per):
            result = jnp.dot(mixed[t], ext[t, window, :], preferred_element_type=F32).astype(BF)
            for p in range(PAIRS):
                column[pl.ds(t * chunk, chunk), pl.ds(p * width, width)] = result[p * chunk : (p + 1) * chunk]
        matched = jnp.dot(column[...], across[...], preferred_element_type=F32)
        for t in range(per):
            sky = science[at, pl.ds(t * tile, tile)]
            diff[t, at, :] = (sky - matched[t * chunk : (t + 1) * chunk]).astype(BF)
        for k in range(slots):
            parcel[k, at, :] = diff[from_low[k] - d * per, at, :]
            parcel[slots + k, at, :] = diff[from_high[k] - d * per, at, :]

            @pl.when(has_low)
            def _():
                chunk_to_low(k, c, low).start()

            @pl.when(has_high)
            def _():
                chunk_to_high(k, c, high).start()

        return carry

    lax.fori_loop(0, chunks, one_chunk, 0)

    def out_copy(j):
        return pltpu.make_async_copy(back.at[j], out_h.at[j], out_sem.at[j])

    def unshift(j, x):
        t = returning[j]
        back[j] = moved(one_hot(tile, margin[1, t]), x, one_hot(tile, -margin[2, t]))
        out_copy(j).start()

    for k in range(slots):
        unshift(slots + k, diff[own_tiles[k] - d * per])
    for k in range(slots):

        @pl.when(has_low)
        def _():
            for c in range(chunks):
                chunk_to_high(k, c, low).wait_recv()
            unshift(k, landed[k])

        @pl.when(has_high)
        def _():
            for c in range(chunks):
                chunk_to_low(k, c, high).wait_recv()
            unshift(2 * slots + k, landed[slots + k])

    for k in range(slots):
        out_copy(slots + k).wait()

    @pl.when(has_low)
    def _():
        for k in range(slots):
            tile_to_low(k, low).wait_send()
            for c in range(chunks):
                chunk_to_low(k, c, low).wait_send()
        halo_to_low(low).wait_send()
        for k in range(slots):
            out_copy(k).wait()

    @pl.when(has_high)
    def _():
        for k in range(slots):
            tile_to_high(k, high).wait_send()
            for c in range(chunks):
                chunk_to_high(k, c, high).wait_send()
        halo_to_high(high).wait_send()
        for k in range(slots):
            out_copy(2 * slots + k).wait()


def mean_kernel(owners, per, owned, slots, margin, arrived_h, out_h, arrived, nothing, sums, load_sem, sems):
    d = lax.axis_index("visit")
    load = pltpu.make_async_copy(arrived_h, arrived, load_sem)
    load.start()
    nothing[...] = jnp.zeros(nothing.shape, F32)
    ids, there = [], []
    for strip in (d - 1, d, d + 1):
        _, local, present = named_tiles(margin, strip, d, owners, per, owned, slots)
        ids += local
        there += present

    def hits_of(p):
        hits = [((ids[j] == p) & (there[j] == 1)) for j in range(3 * slots)]
        return hits, sum(hit.astype(jnp.int32) for hit in hits)

    def zero(p, carry):
        @pl.when(hits_of(p)[1] == 0)
        def _():
            pltpu.make_async_copy(nothing, out_h.at[p], sems.at[p]).start()

        return carry

    lax.fori_loop(0, owned, zero, 0)
    load.wait()

    def patch(p, carry):
        hits, count = hits_of(p)
        scale = 1.0 / jnp.maximum(jnp.full((1, 1), count, jnp.int32).astype(F32), 1.0)
        before = jnp.int32(0)
        for j, hit in enumerate(hits):

            @pl.when(hit & (before == 0))
            def _():
                sums[p] = arrived[j].astype(F32) * scale

            @pl.when(hit & (before > 0))
            def _():
                sums[p] += arrived[j].astype(F32) * scale

            before = before + hit.astype(jnp.int32)

        @pl.when(count > 0)
        def _():
            pltpu.make_async_copy(sums.at[p], out_h.at[p], sems.at[p]).start()

        return carry

    lax.fori_loop(0, owned, patch, 0)

    def finish(p, carry):
        pltpu.make_async_copy(sums.at[p], out_h.at[p], sems.at[p]).wait()
        return carry

    lax.fori_loop(0, owned, finish, 0)


def body(science, patches, margin, kernel_coef, ccd_first):
    owners = lax.axis_size("visit")
    owned, tile = patches.shape[0], patches.shape[1]
    per = science.shape[1] // tile
    slots = per // 2
    chunks = 4
    chunk = tile // chunks
    depth = chunk + 2 * EDGE
    width = tile + SIDE
    smem = pl.BlockSpec(memory_space=pltpu.SMEM)
    anywhere = pl.BlockSpec(memory_space=pl.ANY)
    dma = pltpu.SemaphoreType.DMA
    margin = margin.T
    arrived = pl.pallas_call(
        functools.partial(match_kernel, owners, per, owned, tile, slots),
        out_shape=jax.ShapeDtypeStruct((3 * slots, tile, tile), BF),
        in_specs=[smem, smem, smem, anywhere, anywhere],
        out_specs=anywhere,
        scratch_shapes=[
            pltpu.VMEM((owned, tile, tile), F32),
            pltpu.VMEM((tile, per * tile), F32),
            pltpu.VMEM((2 * slots, tile, tile), BF),
            pltpu.VMEM((3 * slots, tile, tile), BF),
            pltpu.VMEM((3 * slots, tile, tile), BF),
            pltpu.VMEM((per, tile + 2 * EDGE, width), BF),
            pltpu.VMEM((2, per, EDGE, tile), BF),
            pltpu.VMEM((PAIRS, chunk, depth), F32),
            pltpu.VMEM((per, PAIRS * chunk, depth), BF),
            pltpu.VMEM((PAIRS * width, tile), BF),
            pltpu.VMEM((per * chunk, PAIRS * width), BF),
            pltpu.VMEM((per, tile, tile), BF),
            pltpu.VMEM((2 * slots, tile, tile), BF),
            pltpu.VMEM((2 * slots, tile, tile), BF),
            pltpu.VMEM((3 * slots, tile, tile), BF),
            dma((2,)),
            dma((2 * slots,)),
            dma((2 * slots,)),
            dma((2,)),
            dma((2,)),
            dma((chunks, 2 * slots)),
            dma((chunks, 2 * slots)),
            dma((3 * slots,)),
        ],
        compiler_params=pltpu.CompilerParams(
            collective_id=0, has_side_effects=True, vmem_limit_bytes=64 * 1024 * 1024
        ),
        name="match",
    )(margin, kernel_coef.T, ccd_first, patches, science)
    return pl.pallas_call(
        functools.partial(mean_kernel, owners, per, owned, slots),
        out_shape=jax.ShapeDtypeStruct(patches.shape, F32),
        in_specs=[smem, anywhere],
        out_specs=anywhere,
        scratch_shapes=[
            pltpu.VMEM(arrived.shape, BF),
            pltpu.VMEM((tile, tile), F32),
            pltpu.VMEM(patches.shape, F32),
            dma(()),
            dma((owned,)),
        ],
        compiler_params=pltpu.CompilerParams(vmem_limit_bytes=64 * 1024 * 1024),
        name="mean",
    )(margin, arrived)


def solution(mesh):
    in_specs = (
        P(("grp", "visit"), None),
        P(("grp", "visit"), None, None),
        P("grp", None),
        P(None, ("grp", "visit")),
        P("grp"),
    )
    out_specs = P(("grp", "visit"), None, None)
    return jax.shard_map(body, mesh=mesh, in_specs=in_specs, out_specs=out_specs, check_vma=False)
```

time: 33.8 us -> 27.3 us (0.81)
  local copies, waits for them, and re-layouts: 5.01 us -> 0 us
  Pallas kernels: 28.5 us -> 27 us
    unnamed x8 -> x0, local copies, waits for them, and re-layouts: 5.01 us -> none
    pallas_call x1, Pallas kernels: 25.9 us -> 23.6 us  [body(): pl.pallas_call(functools.partial(match_kernel, owners, per, owned, tile,...]
    pallas_call x1, Pallas kernels: 2.61 us -> 3.46 us  [body(): pl.pallas_call(functools.partial(mean_kernel, owners, per, owned, slots),...]
where the time goes in v1:
time: 27.3 us; the launch traced here: 27.1 us
  Pallas kernels  27 us (99%)
    pallas_call x1, Pallas kernels, body(): pl.pallas_call(functools.partial(match_kernel, owners, per, owned, tile,...  23.6 us
    pallas_call x1, Pallas kernels, body(): pl.pallas_call(functools.partial(mean_kernel, owners, per, owned, slots),...  3.46 us

profile of v1, /device:TPU:1, one launch (start us, length us, event | category | flops | bytes accessed | tf_op | source)
XLA Modules:
  0.0 27.1 jit_solution(14618841028319954424)
XLA Ops:
  0.0 23.6 %match.1.arrived_h = bf16[6,256,256]{2,1,0:T(8,128)(2,1)} custom-call(s32[3,64]{1,0:T(4,128)} %bitcast.2, f32[4,27]{1,0:T(4,128)} %bitcast.4, s32[16]{0:T(128)} %ccd.1, f32[8,256,256]{2,1,0:T(8,128)} %patches_h.1, f32[256,1024]{1,0:T(8,128)} %science_h.1), custom_call_target="tpu_custom_call" | custom-call | tf_op jit(solution)/shard_map/match/pallas_call | solution.py:407
  23.6 3.5 %mean.1 = f32[8,256,256]{2,1,0:T(8,128)} custom-call(s32[3,64]{1,0:T(4,128)} %bitcast.3, bf16[6,256,256]{2,1,0:T(8,128)(2,1)} %match.1.arrived_h), custom_call_target="tpu_custom_call" | custom-call | tf_op jit(solution)/shard_map/mean/pallas_call | solution.py:442

commit v2 on v1

v2 whole, which is shorter than its diff:
```python
import functools
import math

import jax
import jax.numpy as jnp
from jax import lax
from jax.experimental import pallas as pl
from jax.experimental.pallas import tpu as pltpu
from jax.sharding import PartitionSpec as P

RADIUS = 10
SIGMAS = 3
ORDERS = 3
PAIRS = SIGMAS * ORDERS
EDGE = 16
SIDE = 128
BF = jnp.bfloat16
F32 = jnp.float32


def sigma_of(g):
    return 0.75 * 2.0**g


def norm_of(g):
    sigma = sigma_of(g)
    return sum(math.exp(-u * u / (2.0 * sigma * sigma)) for u in range(-RADIUS, RADIUS + 1))


def basis_functions(u, g):
    sigma = sigma_of(g)
    inside = jnp.abs(u) <= RADIUS
    base = jnp.where(inside, jnp.exp(u * u * (-1.0 / (2.0 * sigma * sigma))) * (1.0 / norm_of(g)), 0.0)
    scaled = u * (1.0 / sigma)
    first = base * scaled
    return base, first, first * scaled


def named_tiles(margin, strip, owner, owners, per, owned, slots):
    valid = (strip >= 0) & (strip < owners)
    row = (jnp.clip(strip, 0, owners - 1) * per).astype(jnp.int32)
    tiles = [row] * slots
    locals_ = [jnp.int32(0)] * slots
    there = [jnp.int32(0)] * slots
    count = jnp.int32(0)
    for t in range(per):
        patch = margin[0, row + t]
        who = lax.div(patch, jnp.int32(owned))
        named = ((who == owner) & valid).astype(jnp.int32)
        for k in range(slots):
            hit = (named == 1) & (count == k)
            tiles[k] = jnp.where(hit, row + t, tiles[k])
            locals_[k] = jnp.where(hit, patch - who * owned, locals_[k])
            there[k] = jnp.where(hit, jnp.int32(1), there[k])
        count = count + named
    return tiles, locals_, there


def one_hot(size, shift):
    rows = lax.broadcasted_iota(jnp.int32, (size, size), 0)
    cols = lax.broadcasted_iota(jnp.int32, (size, size), 1)
    return jnp.where(((rows - cols + shift) & (size - 1)) == 0, 1.0, 0.0).astype(BF)


def moved(down, x, right):
    a = jnp.dot(down, x, preferred_element_type=F32).astype(BF)
    return jnp.dot(a, right, preferred_element_type=F32).astype(BF)


def match_kernel(
    owners, per, owned, tile, slots,
    margin, ccd, coef, patches_h, science_h,
    out_h,
    patches, science, sky_out, sky, coefs, ext, frame, frames, halo_out, halo, reply, reply_out, replies,
    tab, mixed, across, across_side, column, side_rows, side_column, matched, back,
    load_sem, coef_send, coef_recv, frame_send, frame_recv, halo_send, halo_recv, reply_send, reply_recv,
    sky_send, sky_recv, out_sem,
):
    d = lax.axis_index("visit")
    has_low, has_high = d > 0, d < owners - 1
    low, high = d - 1, d + 1
    chunks = 4
    chunk = tile // chunks
    depth = chunk + 2 * EDGE
    places = 3 * slots

    barrier = pltpu.get_barrier_semaphore()

    @pl.when(has_low)
    def _():
        pl.semaphore_signal(barrier, inc=1, device_id={"visit": low}, device_id_type=pl.DeviceIdType.MESH)

    @pl.when(has_high)
    def _():
        pl.semaphore_signal(barrier, inc=1, device_id={"visit": high}, device_id_type=pl.DeviceIdType.MESH)

    patch_load = pltpu.make_async_copy(patches_h, patches, load_sem.at[0])
    patch_load.start()
    science_loads = [
        pltpu.make_async_copy(science_h.at[:, pl.ds(t * tile, tile)], science.at[t], load_sem.at[1 + t])
        for t in range(per)
    ]
    for load in science_loads:
        load.start()

    high_tiles, high_local, _ = named_tiles(margin, high, d, owners, per, owned, slots)
    low_tiles, low_local, _ = named_tiles(margin, low, d, owners, per, owned, slots)
    own_tiles, own_local, _ = named_tiles(margin, d, d, owners, per, owned, slots)
    from_low, _, _ = named_tiles(margin, d, low, owners, per, owned, slots)
    from_high, _, _ = named_tiles(margin, d, high, owners, per, owned, slots)
    held = low_tiles + own_tiles + high_tiles
    held_local = low_local + own_local + high_local
    first_slot = pl.ds(0, slots)
    last_slot = pl.ds(2 * slots, slots)

    def pair(src_high, dst_high, src_low, dst_low, send, recv, k):
        def to_high(target):
            return pltpu.make_async_remote_copy(
                src_ref=src_high, dst_ref=dst_high, send_sem=send.at[k], recv_sem=recv.at[k],
                device_id={"visit": target}, device_id_type=pl.DeviceIdType.MESH,
            )

        def to_low(target):
            return pltpu.make_async_remote_copy(
                src_ref=src_low, dst_ref=dst_low, send_sem=send.at[k + 1], recv_sem=recv.at[k + 1],
                device_id={"visit": target}, device_id_type=pl.DeviceIdType.MESH,
            )

        def start():
            @pl.when(has_high)
            def _():
                to_high(high).start()

            @pl.when(has_low)
            def _():
                to_low(low).start()

        def arrive():
            @pl.when(has_low)
            def _():
                to_high(low).wait_recv()

            @pl.when(has_high)
            def _():
                to_low(high).wait_recv()

        def sent():
            @pl.when(has_high)
            def _():
                to_high(high).wait_send()

            @pl.when(has_low)
            def _():
                to_low(low).wait_send()

        return start, arrive, sent

    coef_start, coef_arrive, coef_sent = pair(
        coefs.at[1], coefs.at[0], coefs.at[1], coefs.at[2], coef_send, coef_recv, 0
    )
    frame_start, frame_arrive, frame_sent = pair(
        frame.at[last_slot], frames.at[first_slot], frame.at[first_slot], frames.at[last_slot],
        frame_send, frame_recv, 0,
    )
    halo_start, halo_arrive, halo_sent = pair(
        halo_out.at[0], halo.at[0], halo_out.at[1], halo.at[1], halo_send, halo_recv, 0
    )
    reply_start, reply_arrive, reply_sent = pair(
        reply_out.at[1], replies.at[first_slot], reply_out.at[0], replies.at[last_slot], reply_send, reply_recv, 0
    )
    skies = [
        pair(
            sky_out.at[slots + k], sky.at[k], sky_out.at[k], sky.at[2 * slots + k], sky_send, sky_recv, 2 * k
        )
        for k in range(slots)
    ]

    coefs[1] = jnp.zeros(coefs.shape[1:], F32)
    coefs[1, pl.ds(0, coef.shape[0]), pl.ds(0, coef.shape[1])] = coef[...]
    patch_load.wait()
    pl.semaphore_wait(barrier, has_low.astype(jnp.int32) + has_high.astype(jnp.int32))
    coef_start()

    rows = lax.broadcasted_iota(jnp.int32, (2 * EDGE, tile), 0)
    cols = lax.broadcasted_iota(jnp.int32, (2 * EDGE, tile), 1)
    border = jnp.where(cols == jnp.where(rows < EDGE, rows, rows + tile - 2 * EDGE), 1.0, 0.0).astype(BF)
    for j in range(places):
        t = held[j]
        x = moved(one_hot(tile, -margin[1, t]), patches[held_local[j]].astype(BF), one_hot(tile, margin[2, t]))
        ext[j, pl.ds(EDGE, tile), pl.ds(0, tile)] = x
        frame[j, pl.ds(0, EDGE), :] = x[:EDGE]
        frame[j, pl.ds(EDGE, EDGE), :] = x[tile - EDGE :]
        frame[j, pl.ds(2 * EDGE, 2 * EDGE), :] = lax.dot_general(
            border, x, (((1,), (1,)), ((), ())), preferred_element_type=F32
        ).astype(BF)
    frame_start()
    for k in range(slots):
        frames[slots + k] = frame[slots + k]

    for load in science_loads:
        load.wait()
    for k in range(slots):
        sky_out[k] = science[from_low[k] - d * per].astype(BF)
        sky_out[slots + k] = science[from_high[k] - d * per].astype(BF)
        sky[slots + k] = science[own_tiles[k] - d * per].astype(BF)
    skies[0][0]()

    rows = lax.broadcasted_iota(jnp.int32, (chunk, depth), 0)
    cols = lax.broadcasted_iota(jnp.int32, (chunk, depth), 1)
    u = (cols - rows - EDGE).astype(F32)
    for g in range(SIGMAS):
        for v, table in enumerate(basis_functions(u, g)):
            tab[g * ORDERS + v] = table

    def across_rows(b, carry):
        r = lax.broadcasted_iota(jnp.int32, (SIDE, tile), 0)
        c = lax.broadcasted_iota(jnp.int32, (SIDE, tile), 1)
        side = jnp.where(r < SIDE // 2, r + tile, r - SIDE)
        main = b * SIDE < tile
        w = (jnp.where(main, r + b * SIDE, side) - c).astype(F32)
        for g in range(SIGMAS):
            for h, table in enumerate(basis_functions(w, g)):
                p = g * ORDERS + h
                table = table.astype(BF)

                @pl.when(main)
                def _():
                    across[pl.ds(pl.multiple_of(p * tile + b * SIDE, SIDE), SIDE), :] = table

                @pl.when(jnp.logical_not(main))
                def _():
                    across_side[pl.ds(p * SIDE, SIDE), :] = table

        return carry

    lax.fori_loop(0, tile // SIDE + 1, across_rows, 0)

    coef_arrive()
    for j in range(places):
        of = j // slots
        start = jnp.clip(d + of - 1, 0, owners - 1) * per
        weights = coefs[of, pl.ds(held[j] - start, 1), :]
        for g in range(SIGMAS):
            for h in range(ORDERS):
                p = g * ORDERS + h
                total = weights[:, p * ORDERS : p * ORDERS + 1] * tab[g * ORDERS]
                for v in range(1, ORDERS):
                    at = p * ORDERS + v
                    total = total + weights[:, at : at + 1] * tab[g * ORDERS + v]
                mixed[j, pl.ds(p * chunk, chunk), :] = total.astype(BF)

    who = [lax.div(margin[0, d * per + t], jnp.int32(owned)) for t in range(per)]
    place = []
    for t in range(per):
        rank = jnp.int32(0)
        for s in range(t):
            rank = rank + (who[s] == who[t]).astype(jnp.int32)
        place.append(jnp.clip((who[t] - d + 1) * slots + rank, 0, places - 1))

    frame_arrive()
    for t in range(per):
        f = frames[place[t]]
        halo_out[0, t] = f[EDGE : 2 * EDGE]
        halo_out[1, t] = f[:EDGE]
        reply[t, pl.ds(2 * EDGE, 2 * EDGE), pl.ds(tile, SIDE)] = jnp.zeros((2 * EDGE, SIDE), BF)
        if t + 1 < per:
            reply[t + 1, pl.ds(2 * EDGE, EDGE), pl.ds(0, tile)] = f[3 * EDGE :]
        if t > 0:
            reply[t - 1, pl.ds(3 * EDGE, EDGE), pl.ds(0, tile)] = f[2 * EDGE : 3 * EDGE]
    reply[0, pl.ds(2 * EDGE, EDGE), pl.ds(0, tile)] = jnp.zeros((EDGE, tile), BF)
    reply[per - 1, pl.ds(3 * EDGE, EDGE), pl.ds(0, tile)] = jnp.zeros((EDGE, tile), BF)
    halo_start()

    def hand_back():
        halo_arrive()
        keep = (
            has_low & (ccd[d] == 0),
            has_high & (ccd[jnp.minimum(d + 1, owners - 1)] == 0),
        )
        nothing = jnp.zeros((EDGE, tile), BF)
        lane = lax.broadcasted_iota(jnp.int32, (EDGE, SIDE), 1)
        none = jnp.zeros((EDGE, SIDE), F32)
        for i in range(2):
            parts = [jnp.where(keep[i], halo[i, t], nothing) for t in range(per)]
            for t in range(per):
                right = parts[t + 1][:, :SIDE].astype(F32) if t + 1 < per else none
                left = parts[t - 1][:, tile - SIDE :].astype(F32) if t > 0 else none
                at = pl.ds(i * EDGE, EDGE)
                reply[t, at, pl.ds(0, tile)] = parts[t]
                reply[t, at, pl.ds(tile, SIDE)] = jnp.where(lane < SIDE // 2, right, left).astype(BF)
        for k in range(slots):
            reply_out[0, k] = reply[from_low[k] - d * per]
            reply_out[1, k] = reply[from_high[k] - d * per]
            replies[slots + k] = reply[own_tiles[k] - d * per]
        reply_start()
        for k in range(1, slots):
            skies[k][0]()

    def surround():
        reply_arrive()
        r = lax.broadcasted_iota(jnp.int32, (2 * EDGE, SIDE), 0)
        c = lax.broadcasted_iota(jnp.int32, (2 * EDGE, SIDE), 1)
        spread = jnp.where(c == jnp.where(r < EDGE, r + SIDE - EDGE, r - EDGE), 1.0, 0.0).astype(BF)
        for j in range(places):
            ext[j, pl.ds(0, EDGE), :] = replies[j, pl.ds(0, EDGE), :]
            ext[j, pl.ds(EDGE + tile, EDGE), :] = replies[j, pl.ds(EDGE, EDGE), :]
            ext[j, pl.ds(EDGE, tile), pl.ds(tile, SIDE)] = lax.dot_general(
                replies[j, pl.ds(2 * EDGE, 2 * EDGE), pl.ds(0, tile)], spread,
                (((0,), (0,)), ((), ())), preferred_element_type=F32,
            ).astype(BF)

    def one_chunk(i, carry):
        c = lax.rem(i + 1, chunks)

        @pl.when(i == 1)
        def _():
            hand_back()

        @pl.when(i == chunks - 2)
        def _():
            surround()

        window = pl.ds(pl.multiple_of(c * chunk, chunk), depth)
        for j in range(places):
            result = jnp.dot(mixed[j], ext[j, window, pl.ds(0, tile)], preferred_element_type=F32).astype(BF)
            for p in range(PAIRS):
                column[pl.ds(j * chunk, chunk), pl.ds(p * tile, tile)] = result[p * chunk : (p + 1) * chunk]
        matched[c] = jnp.dot(column[...], across[...], preferred_element_type=F32)
        return carry

    lax.fori_loop(0, chunks, one_chunk, 0)

    for j in range(places):
        for c in range(chunks):
            side_rows[j, :, pl.ds(c * SIDE, SIDE)] = ext[j, pl.ds(c * chunk, depth), pl.ds(tile, SIDE)]

    def side_tile(j, carry):
        result = jnp.dot(mixed[j], side_rows[j], preferred_element_type=F32).astype(BF)
        for c in range(chunks):
            start = pl.multiple_of((j * chunks + c) * chunk, chunk)
            for p in range(PAIRS):
                side_column[pl.ds(start, chunk), pl.ds(p * SIDE, SIDE)] = result[
                    p * chunk : (p + 1) * chunk, c * SIDE : (c + 1) * SIDE
                ]
        return carry

    lax.fori_loop(0, places, side_tile, 0, unroll=2)
    for start, arrive, sent in skies:
        arrive()

    def out_copy(j):
        return pltpu.make_async_copy(back.at[j], out_h.at[j], out_sem.at[j])

    for j in range(places):
        sides = jnp.dot(
            side_column[pl.ds(j * tile, tile), :], across_side[...], preferred_element_type=F32
        )
        whole = jnp.concatenate([matched[c, pl.ds(j * chunk, chunk), :] for c in range(chunks)], axis=0)
        diff = (sky[j].astype(F32) - (whole + sides)).astype(BF)
        t = held[j]
        back[j] = moved(one_hot(tile, margin[1, t]), diff, one_hot(tile, -margin[2, t]))
        out_copy(j).start()

    for j in range(places):
        out_copy(j).wait()
    for sent in [coef_sent, frame_sent, halo_sent, reply_sent] + [sky_pair[2] for sky_pair in skies]:
        sent()


def mean_kernel(owners, per, owned, slots, margin, arrived_h, out_h, arrived, nothing, sums, load_sem, sems):
    d = lax.axis_index("visit")
    load = pltpu.make_async_copy(arrived_h, arrived, load_sem)
    load.start()
    nothing[...] = jnp.zeros(nothing.shape, F32)
    ids, there = [], []
    for strip in (d - 1, d, d + 1):
        _, local, present = named_tiles(margin, strip, d, owners, per, owned, slots)
        ids += local
        there += present

    def hits_of(p):
        hits = [((ids[j] == p) & (there[j] == 1)) for j in range(3 * slots)]
        return hits, sum(hit.astype(jnp.int32) for hit in hits)

    def zero(p, carry):
        @pl.when(hits_of(p)[1] == 0)
        def _():
            pltpu.make_async_copy(nothing, out_h.at[p], sems.at[p]).start()

        return carry

    lax.fori_loop(0, owned, zero, 0)
    load.wait()

    def patch(p, carry):
        hits, count = hits_of(p)
        scale = 1.0 / jnp.maximum(jnp.full((1, 1), count, jnp.int32).astype(F32), 1.0)
        before = jnp.int32(0)
        for j, hit in enumerate(hits):

            @pl.when(hit & (before == 0))
            def _():
                sums[p] = arrived[j].astype(F32) * scale

            @pl.when(hit & (before > 0))
            def _():
                sums[p] += arrived[j].astype(F32) * scale

            before = before + hit.astype(jnp.int32)

        @pl.when(count > 0)
        def _():
            pltpu.make_async_copy(sums.at[p], out_h.at[p], sems.at[p]).start()

        return carry

    lax.fori_loop(0, owned, patch, 0)

    def finish(p, carry):
        pltpu.make_async_copy(sums.at[p], out_h.at[p], sems.at[p]).wait()
        return carry

    lax.fori_loop(0, owned, finish, 0)


def body(science, patches, margin, kernel_coef, ccd_first):
    owners = lax.axis_size("visit")
    owned, tile = patches.shape[0], patches.shape[1]
    per = science.shape[1] // tile
    slots = per // 2
    chunks = 4
    chunk = tile // chunks
    depth = chunk + 2 * EDGE
    width = tile + SIDE
    smem = pl.BlockSpec(memory_space=pltpu.SMEM)
    anywhere = pl.BlockSpec(memory_space=pl.ANY)
    dma = pltpu.SemaphoreType.DMA
    margin = margin.T
    places = 3 * slots
    arrived = pl.pallas_call(
        functools.partial(match_kernel, owners, per, owned, tile, slots),
        out_shape=jax.ShapeDtypeStruct((places, tile, tile), BF),
        in_specs=[smem, smem, pl.BlockSpec(memory_space=pltpu.VMEM), anywhere, anywhere],
        out_specs=anywhere,
        scratch_shapes=[
            pltpu.VMEM((owned, tile, tile), F32),
            pltpu.VMEM((per, tile, tile), F32),
            pltpu.VMEM((2 * slots, tile, tile), BF),
            pltpu.VMEM((places, tile, tile), BF),
            pltpu.VMEM((3, -(-per // 8) * 8, 128), F32),
            pltpu.VMEM((places, tile + 2 * EDGE, width), BF),
            pltpu.VMEM((places, 4 * EDGE, tile), BF),
            pltpu.VMEM((places, 4 * EDGE, tile), BF),
            pltpu.VMEM((2, per, EDGE, tile), BF),
            pltpu.VMEM((2, per, EDGE, tile), BF),
            pltpu.VMEM((per, 4 * EDGE, width), BF),
            pltpu.VMEM((2, slots, 4 * EDGE, width), BF),
            pltpu.VMEM((places, 4 * EDGE, width), BF),
            pltpu.VMEM((PAIRS, chunk, depth), F32),
            pltpu.VMEM((places, PAIRS * chunk, depth), BF),
            pltpu.VMEM((PAIRS * tile, tile), BF),
            pltpu.VMEM((PAIRS * SIDE, tile), BF),
            pltpu.VMEM((places * chunk, PAIRS * tile), BF),
            pltpu.VMEM((places, depth, chunks * SIDE), BF),
            pltpu.VMEM((places * tile, PAIRS * SIDE), BF),
            pltpu.VMEM((chunks, places * chunk, tile), F32),
            pltpu.VMEM((places, tile, tile), BF),
            dma((1 + per,)),
            dma((2,)),
            dma((2,)),
            dma((2,)),
            dma((2,)),
            dma((2,)),
            dma((2,)),
            dma((2,)),
            dma((2,)),
            dma((2 * slots,)),
            dma((2 * slots,)),
            dma((places,)),
        ],
        compiler_params=pltpu.CompilerParams(
            collective_id=0, has_side_effects=True, vmem_limit_bytes=64 * 1024 * 1024
        ),
        name="match",
    )(margin, ccd_first, kernel_coef.T, patches, science)
    return pl.pallas_call(
        functools.partial(mean_kernel, owners, per, owned, slots),
        out_shape=jax.ShapeDtypeStruct(patches.shape, F32),
        in_specs=[smem, anywhere],
        out_specs=anywhere,
        scratch_shapes=[
            pltpu.VMEM(arrived.shape, BF),
            pltpu.VMEM((tile, tile), F32),
            pltpu.VMEM(patches.shape, F32),
            dma(()),
            dma((owned,)),
        ],
        compiler_params=pltpu.CompilerParams(vmem_limit_bytes=64 * 1024 * 1024),
        name="mean",
    )(margin, arrived)


def solution(mesh):
    in_specs = (
        P(("grp", "visit"), None),
        P(("grp", "visit"), None, None),
        P("grp", None),
        P(None, ("grp", "visit")),
        P("grp"),
    )
    out_specs = P(("grp", "visit"), None, None)
    return jax.shard_map(body, mesh=mesh, in_specs=in_specs, out_specs=out_specs, check_vma=False)
```

time: 27.3 us -> 30.5 us (1.12)
  the two profiles are of different devices: /device:TPU:1 before, /device:TPU:25 now
where the time goes in v2:
time: 30.5 us; the launch traced here: 30.2 us
  Pallas kernels  30.2 us (99%)
    pallas_call x1, Pallas kernels, body(): pl.pallas_call(functools.partial(match_kernel, owners, per, owned, tile,...  26.7 us
    pallas_call x1, Pallas kernels, body(): pl.pallas_call(functools.partial(mean_kernel, owners, per, owned, slots),...  3.43 us

profile of v2, /device:TPU:25, one launch (start us, length us, event | category | flops | bytes accessed | tf_op | source)
XLA Modules:
  0.0 30.2 jit_solution(8999046862269580490)
XLA Ops:
  0.0 26.7 %match.1.arrived_h = bf16[6,256,256]{2,1,0:T(8,128)(2,1)} custom-call(s32[3,64]{1,0:T(4,128)} %bitcast.2, s32[16]{0:T(128)} %ccd.1, f32[4,27]{1,0:T(4,128)} %bitcast.4, f32[8,256,256]{2,1,0:T(8,128)} %patches_h.1, f32[256,1024]{1,0:T(8,128)} %science_h.1), custom_call_target="tpu_custom_call" | custom-call | tf_op jit(solution)/shard_map/match/pallas_call | solution.py:440
  26.7 3.4 %mean.1 = f32[8,256,256]{2,1,0:T(8,128)} custom-call(s32[3,64]{1,0:T(4,128)} %bitcast.3, bf16[6,256,256]{2,1,0:T(8,128)(2,1)} %match.1.arrived_h), custom_call_target="tpu_custom_call" | custom-call | tf_op jit(solution)/shard_map/mean/pallas_call | solution.py:486

commit v3 on v1

--- a/solution.py
+++ b/solution.py
@@ -69,9 +69,9 @@
 
 def match_kernel(
     owners, per, owned, tile, slots,
-    margin, coef, ccd, patches_h, science_h,
-    out_h,
-    patches, science, stage, pool, forth, ext, halo, tab, mixed, across, column, diff, parcel, landed, back,
+    margin_h, coef_h, ccd_h, patches_h, science_h,
+    out,
+    margin, coef, ccd, patches, science, stage, pool, ext, halo, tab, mixed, across, column, diff, parcel, back,
     load_sem, tile_send, tile_recv, halo_send, halo_recv, back_send, back_recv, out_sem,
 ):
     d = lax.axis_index("visit")
@@ -95,16 +95,21 @@
 
     patch_load = pltpu.make_async_copy(patches_h, patches, load_sem.at[0])
     science_load = pltpu.make_async_copy(science_h, science, load_sem.at[1])
+    margin_load = pltpu.make_async_copy(margin_h, margin, load_sem.at[2])
+    coef_load = pltpu.make_async_copy(coef_h, coef, load_sem.at[3])
+    ccd_load = pltpu.make_async_copy(ccd_h, ccd, load_sem.at[4])
+    margin_load.start()
     patch_load.start()
+    coef_load.start()
+    ccd_load.start()
     science_load.start()
+    margin_load.wait()
 
     high_tiles, high_local, _ = named_tiles(margin, high, d, owners, per, owned, slots)
     low_tiles, low_local, _ = named_tiles(margin, low, d, owners, per, owned, slots)
     own_tiles, own_local, _ = named_tiles(margin, d, d, owners, per, owned, slots)
     from_low, _, _ = named_tiles(margin, d, low, owners, per, owned, slots)
     from_high, _, _ = named_tiles(margin, d, high, owners, per, owned, slots)
-    arriving = from_low + own_tiles + from_high
-    returning = low_tiles + own_tiles + high_tiles
 
     def remote(src, dst, send, recv, target):
         return pltpu.make_async_remote_copy(
@@ -119,27 +124,28 @@
         j = slots + k
         return remote(stage.at[j], pool.at[2 * slots + k], tile_send.at[j], tile_recv.at[j], target)
 
+    def aligned(t, local):
+        return moved(one_hot(tile, -margin[1, t]), patches[local].astype(BF), one_hot(tile, margin[2, t]))
+
     patch_load.wait()
     for k in range(slots):
-        stage[k] = patches[high_local[k]].astype(BF)
-        stage[slots + k] = patches[low_local[k]].astype(BF)
-    pl.semaphore_wait(barrier, has_low.astype(jnp.int32) + has_high.astype(jnp.int32))
+        stage[k] = aligned(high_tiles[k], high_local[k])
+        stage[slots + k] = aligned(low_tiles[k], low_local[k])
+        if k == 0:
+            pl.semaphore_wait(barrier, has_low.astype(jnp.int32) + has_high.astype(jnp.int32))
+
+        @pl.when(has_high)
+        def _():
+            tile_to_high(k, high).start()
+
+        @pl.when(has_low)
+        def _():
+            tile_to_low(k, low).start()
+
     for k in range(slots):
-
-        @pl.when(has_high)
-        def _():
-            tile_to_high(k, high).start()
-
-        @pl.when(has_low)
-        def _():
-            tile_to_low(k, low).start()
-
-    for k in range(slots):
-        pool[slots + k] = patches[own_local[k]].astype(BF)
-
-    def align(j):
-        t = arriving[j]
-        forth[j] = moved(one_hot(tile, -margin[1, t]), pool[j], one_hot(tile, margin[2, t]))
+        pool[slots + k] = aligned(own_tiles[k], own_local[k])
+    coef_load.wait()
+    ccd_load.wait()
 
     rows = lax.broadcasted_iota(jnp.int32, (chunk, depth), 0)
     cols = lax.broadcasted_iota(jnp.int32, (chunk, depth), 1)
@@ -173,9 +179,6 @@
 
     lax.fori_loop(0, width // SIDE, across_rows, 0)
 
-    for k in range(slots):
-        align(slots + k)
-
     who = [lax.div(margin[0, d * per + t], jnp.int32(owned)) for t in range(per)]
     place = []
     for t in range(per):
@@ -189,15 +192,13 @@
         @pl.when(has_low)
         def _():
             tile_to_high(k, low).wait_recv()
-            align(k)
 
         @pl.when(has_high)
         def _():
             tile_to_low(k, high).wait_recv()
-            align(2 * slots + k)
 
     for t in range(per):
-        ext[t, pl.ds(EDGE, tile), pl.ds(0, tile)] = forth[place[t]]
+        ext[t, pl.ds(EDGE, tile), pl.ds(0, tile)] = pool[place[t]]
 
     def halo_to_high(target):
         return remote(
@@ -231,13 +232,13 @@
     def chunk_to_low(k, c, target):
         at = pl.ds(pl.multiple_of(c * chunk, chunk), chunk)
         return remote(
-            parcel.at[k, at], landed.at[slots + k, at], back_send.at[c, k], back_recv.at[c, k], target
+            parcel.at[k, at], out.at[2 * slots + k, at], back_send.at[c, k], back_recv.at[c, k], target
         )
 
     def chunk_to_high(k, c, target):
         j = slots + k
         at = pl.ds(pl.multiple_of(c * chunk, chunk), chunk)
-        return remote(parcel.at[j, at], landed.at[k, at], back_send.at[c, j], back_recv.at[c, j], target)
+        return remote(parcel.at[j, at], out.at[k, at], back_send.at[c, j], back_recv.at[c, j], target)
 
     def one_chunk(i, carry):
         c = lax.rem(i + 1, chunks)
@@ -287,32 +288,13 @@
 
     lax.fori_loop(0, chunks, one_chunk, 0)
 
-    def out_copy(j):
-        return pltpu.make_async_copy(back.at[j], out_h.at[j], out_sem.at[j])
-
-    def unshift(j, x):
-        t = returning[j]
-        back[j] = moved(one_hot(tile, margin[1, t]), x, one_hot(tile, -margin[2, t]))
-        out_copy(j).start()
+    def own_copy(k):
+        return pltpu.make_async_copy(back.at[k], out.at[slots + k], out_sem.at[k])
 
     for k in range(slots):
-        unshift(slots + k, diff[own_tiles[k] - d * per])
-    for k in range(slots):
-
-        @pl.when(has_low)
-        def _():
-            for c in range(chunks):
-                chunk_to_high(k, c, low).wait_recv()
-            unshift(k, landed[k])
-
-        @pl.when(has_high)
-        def _():
-            for c in range(chunks):
-                chunk_to_low(k, c, high).wait_recv()
-            unshift(2 * slots + k, landed[slots + k])
-
-    for k in range(slots):
-        out_copy(slots + k).wait()
+        t = own_tiles[k]
+        back[k] = moved(one_hot(tile, margin[1, t]), diff[t - d * per], one_hot(tile, -margin[2, t]))
+        own_copy(k).start()
 
     @pl.when(has_low)
     def _():
@@ -321,8 +303,6 @@
             for c in range(chunks):
                 chunk_to_low(k, c, low).wait_send()
         halo_to_low(low).wait_send()
-        for k in range(slots):
-            out_copy(k).wait()
 
     @pl.when(has_high)
     def _():
@@ -331,27 +311,46 @@
             for c in range(chunks):
                 chunk_to_high(k, c, high).wait_send()
         halo_to_high(high).wait_send()
-        for k in range(slots):
-            out_copy(2 * slots + k).wait()
-
-
-def mean_kernel(owners, per, owned, slots, margin, arrived_h, out_h, arrived, nothing, sums, load_sem, sems):
+
+    for k in range(slots):
+        own_copy(k).wait()
+
+    @pl.when(has_low)
+    def _():
+        for k in range(slots):
+            for c in range(chunks):
+                chunk_to_high(k, c, low).wait_recv()
+
+    @pl.when(has_high)
+    def _():
+        for k in range(slots):
+            for c in range(chunks):
+                chunk_to_low(k, c, high).wait_recv()
+
+
+def mean_kernel(
+    owners, per, owned, slots, margin_h, arrived_h, out_h, margin, arrived, nothing, sums, load_sem, sems
+):
     d = lax.axis_index("visit")
-    load = pltpu.make_async_copy(arrived_h, arrived, load_sem)
+    tile = nothing.shape[0]
+    margin_load = pltpu.make_async_copy(margin_h, margin, load_sem.at[1])
+    margin_load.start()
+    load = pltpu.make_async_copy(arrived_h, arrived, load_sem.at[0])
     load.start()
     nothing[...] = jnp.zeros(nothing.shape, F32)
-    ids, there = [], []
+    margin_load.wait()
+    tiles, ids, there = [], [], []
     for strip in (d - 1, d, d + 1):
-        _, local, present = named_tiles(margin, strip, d, owners, per, owned, slots)
+        named, local, present = named_tiles(margin, strip, d, owners, per, owned, slots)
+        tiles += named
         ids += local
         there += present
 
-    def hits_of(p):
-        hits = [((ids[j] == p) & (there[j] == 1)) for j in range(3 * slots)]
-        return hits, sum(hit.astype(jnp.int32) for hit in hits)
+    def count_of(p):
+        return sum(((ids[j] == p) & (there[j] == 1)).astype(jnp.int32) for j in range(3 * slots))
 
     def zero(p, carry):
-        @pl.when(hits_of(p)[1] == 0)
+        @pl.when(count_of(p) == 0)
         def _():
             pltpu.make_async_copy(nothing, out_h.at[p], sems.at[p]).start()
 
@@ -360,29 +359,34 @@
     lax.fori_loop(0, owned, zero, 0)
     load.wait()
 
-    def patch(p, carry):
-        hits, count = hits_of(p)
-        scale = 1.0 / jnp.maximum(jnp.full((1, 1), count, jnp.int32).astype(F32), 1.0)
-        before = jnp.int32(0)
-        for j, hit in enumerate(hits):
-
-            @pl.when(hit & (before == 0))
-            def _():
-                sums[p] = arrived[j].astype(F32) * scale
-
-            @pl.when(hit & (before > 0))
-            def _():
-                sums[p] += arrived[j].astype(F32) * scale
-
-            before = before + hit.astype(jnp.int32)
-
-        @pl.when(count > 0)
-        def _():
-            pltpu.make_async_copy(sums.at[p], out_h.at[p], sems.at[p]).start()
-
-        return carry
-
-    lax.fori_loop(0, owned, patch, 0)
+    for j in list(range(slots, 2 * slots)) + list(range(slots)) + list(range(2 * slots, 3 * slots)):
+        order = list(range(slots, 2 * slots)) + list(range(slots)) + list(range(2 * slots, 3 * slots))
+        at = order.index(j)
+        p = ids[j]
+        same = [((ids[i] == p) & (there[i] == 1)).astype(jnp.int32) for i in order]
+        before = sum(same[:at], jnp.int32(0))
+        after = sum(same[at + 1 :], jnp.int32(0))
+
+        @pl.when(there[j] == 1)
+        def _():
+            x = arrived[j]
+            if not slots <= j < 2 * slots:
+                t = tiles[j]
+                x = moved(one_hot(tile, margin[1, t]), x, one_hot(tile, -margin[2, t]))
+            count = jnp.full((1, 1), before + after + 1, jnp.int32).astype(F32)
+            value = x.astype(F32) * (1.0 / count)
+
+            @pl.when(before == 0)
+            def _():
+                sums[p] = value
+
+            @pl.when(before > 0)
+            def _():
+                sums[p] += value
+
+            @pl.when(after == 0)
+            def _():
+                pltpu.make_async_copy(sums.at[p], out_h.at[p], sems.at[p]).start()
 
     def finish(p, carry):
         pltpu.make_async_copy(sums.at[p], out_h.at[p], sems.at[p]).wait()
@@ -400,20 +404,22 @@
     chunk = tile // chunks
     depth = chunk + 2 * EDGE
     width = tile + SIDE
-    smem = pl.BlockSpec(memory_space=pltpu.SMEM)
     anywhere = pl.BlockSpec(memory_space=pl.ANY)
+    hbm = pl.BlockSpec(memory_space=pltpu.HBM)
     dma = pltpu.SemaphoreType.DMA
     margin = margin.T
     arrived = pl.pallas_call(
         functools.partial(match_kernel, owners, per, owned, tile, slots),
         out_shape=jax.ShapeDtypeStruct((3 * slots, tile, tile), BF),
-        in_specs=[smem, smem, smem, anywhere, anywhere],
+        in_specs=[hbm] * 5,
         out_specs=anywhere,
         scratch_shapes=[
+            pltpu.SMEM(margin.shape, jnp.int32),
+            pltpu.SMEM(kernel_coef.shape[::-1], F32),
+            pltpu.SMEM(ccd_first.shape, jnp.int32),
             pltpu.VMEM((owned, tile, tile), F32),
             pltpu.VMEM((tile, per * tile), F32),
             pltpu.VMEM((2 * slots, tile, tile), BF),
-            pltpu.VMEM((3 * slots, tile, tile), BF),
             pltpu.VMEM((3 * slots, tile, tile), BF),
             pltpu.VMEM((per, tile + 2 * EDGE, width), BF),
             pltpu.VMEM((2, per, EDGE, tile), BF),
@@ -423,35 +429,35 @@
             pltpu.VMEM((per * chunk, PAIRS * width), BF),
             pltpu.VMEM((per, tile, tile), BF),
             pltpu.VMEM((2 * slots, tile, tile), BF),
-            pltpu.VMEM((2 * slots, tile, tile), BF),
-            pltpu.VMEM((3 * slots, tile, tile), BF),
-            dma((2,)),
+            pltpu.VMEM((slots, tile, tile), BF),
+            dma((5,)),
             dma((2 * slots,)),
             dma((2 * slots,)),
             dma((2,)),
             dma((2,)),
             dma((chunks, 2 * slots)),
             dma((chunks, 2 * slots)),
-            dma((3 * slots,)),
+            dma((slots,)),
         ],
         compiler_params=pltpu.CompilerParams(
-            collective_id=0, has_side_effects=True, vmem_limit_bytes=64 * 1024 * 1024
+            collective_id=0, has_side_effects=True, vmem_limit_bytes=64 * 1024 * 1024 - 3 * slots * tile * tile * 2
         ),
         name="match",
     )(margin, kernel_coef.T, ccd_first, patches, science)
     return pl.pallas_call(
         functools.partial(mean_kernel, owners, per, owned, slots),
         out_shape=jax.ShapeDtypeStruct(patches.shape, F32),
-        in_specs=[smem, anywhere],
-        out_specs=anywhere,
+        in_specs=[hbm, anywhere],
+        out_specs=hbm,
         scratch_shapes=[
+            pltpu.SMEM(margin.shape, jnp.int32),
             pltpu.VMEM(arrived.shape, BF),
             pltpu.VMEM((tile, tile), F32),
             pltpu.VMEM(patches.shape, F32),
-            dma(()),
+            dma((2,)),
             dma((owned,)),
         ],
-        compiler_params=pltpu.CompilerParams(vmem_limit_bytes=64 * 1024 * 1024),
+        compiler_params=pltpu.CompilerParams(vmem_limit_bytes=64 * 1024 * 1024 - 3 * slots * tile * tile * 2),
         name="mean",
     )(margin, arrived)
 

time: 27.3 us -> 24.3 us (0.89)
  Pallas kernels: 27 us -> 24 us
    pallas_call x1, Pallas kernels: 23.6 us -> 21 us  [body(): pl.pallas_call(functools.partial(match_kernel, owners, per, owned, tile,...]
    pallas_call x1, Pallas kernels: 3.46 us -> 3 us  [body(): pl.pallas_call(functools.partial(mean_kernel, owners, per, owned, slots),...]
where the time goes in v3:
time: 24.3 us; the launch traced here: 24 us
  Pallas kernels  24 us (99%)
    pallas_call x1, Pallas kernels, body(): pl.pallas_call(functools.partial(match_kernel, owners, per, owned, tile,...  21 us
    pallas_call x1, Pallas kernels, body(): pl.pallas_call(functools.partial(mean_kernel, owners, per, owned, slots),...  3 us

profile of v3, /device:TPU:1, one launch (start us, length us, event | category | flops | bytes accessed | tf_op | source)
XLA Modules:
  0.0 24.0 jit_solution(9039663375138518458)
XLA Ops:
  0.0 21.0 %match.1.arrived_h = bf16[6,256,256]{2,1,0:T(8,128)(2,1)} custom-call(s32[3,64]{1,0:T(4,128)} %bitcast.2, f32[4,27]{1,0:T(4,128)} %bitcast.4, s32[16]{0:T(128)} %ccd_h.1, f32[8,256,256]{2,1,0:T(8,128)} %patches_h.1, f32[256,1024]{1,0:T(8,128)} %science_h.1), custom_call_target="tpu_custom_call" | custom-call | tf_op jit(solution)/shard_map/match/pallas_call | solution.py:411
  21.0 3.0 %mean.1 = f32[8,256,256]{2,1,0:T(8,128)} custom-call(s32[3,64]{1,0:T(4,128)} %bitcast.3, bf16[6,256,256]{2,1,0:T(8,128)(2,1)} %match.1.arrived_h), custom_call_target="tpu_custom_call" | custom-call | tf_op jit(solution)/shard_map/mean/pallas_call | solution.py:447

commit v4 on v3

--- a/solution.py
+++ b/solution.py
@@ -127,44 +127,12 @@
     def aligned(t, local):
         return moved(one_hot(tile, -margin[1, t]), patches[local].astype(BF), one_hot(tile, margin[2, t]))
 
-    patch_load.wait()
-    for k in range(slots):
-        stage[k] = aligned(high_tiles[k], high_local[k])
-        stage[slots + k] = aligned(low_tiles[k], low_local[k])
-        if k == 0:
-            pl.semaphore_wait(barrier, has_low.astype(jnp.int32) + has_high.astype(jnp.int32))
-
-        @pl.when(has_high)
-        def _():
-            tile_to_high(k, high).start()
-
-        @pl.when(has_low)
-        def _():
-            tile_to_low(k, low).start()
-
-    for k in range(slots):
-        pool[slots + k] = aligned(own_tiles[k], own_local[k])
-    coef_load.wait()
-    ccd_load.wait()
-
     rows = lax.broadcasted_iota(jnp.int32, (chunk, depth), 0)
     cols = lax.broadcasted_iota(jnp.int32, (chunk, depth), 1)
     u = (cols - rows - EDGE).astype(F32)
     for g in range(SIGMAS):
         for v, table in enumerate(basis_functions(u, g)):
             tab[g * ORDERS + v] = table
-
-    def mix_tile(t, carry):
-        for g in range(SIGMAS):
-            for h in range(ORDERS):
-                p = g * ORDERS + h
-                total = coef[t, p * ORDERS] * tab[g * ORDERS]
-                for v in range(1, ORDERS):
-                    total = total + coef[t, p * ORDERS + v] * tab[g * ORDERS + v]
-                mixed[t, pl.ds(p * chunk, chunk), :] = total.astype(BF)
-        return carry
-
-    lax.fori_loop(0, per, mix_tile, 0)
 
     def across_rows(b, carry):
         r = lax.broadcasted_iota(jnp.int32, (SIDE, tile), 0)
@@ -179,6 +147,38 @@
 
     lax.fori_loop(0, width // SIDE, across_rows, 0)
 
+    patch_load.wait()
+    for k in range(slots):
+        stage[k] = aligned(high_tiles[k], high_local[k])
+        stage[slots + k] = aligned(low_tiles[k], low_local[k])
+        if k == 0:
+            pl.semaphore_wait(barrier, has_low.astype(jnp.int32) + has_high.astype(jnp.int32))
+
+        @pl.when(has_high)
+        def _():
+            tile_to_high(k, high).start()
+
+        @pl.when(has_low)
+        def _():
+            tile_to_low(k, low).start()
+
+    for k in range(slots):
+        pool[slots + k] = aligned(own_tiles[k], own_local[k])
+    coef_load.wait()
+    ccd_load.wait()
+
+    def mix_tile(t, carry):
+        for g in range(SIGMAS):
+            for h in range(ORDERS):
+                p = g * ORDERS + h
+                total = coef[t, p * ORDERS] * tab[g * ORDERS]
+                for v in range(1, ORDERS):
+                    total = total + coef[t, p * ORDERS + v] * tab[g * ORDERS + v]
+                mixed[t, pl.ds(p * chunk, chunk), :] = total.astype(BF)
+        return carry
+
+    lax.fori_loop(0, per, mix_tile, 0)
+
     who = [lax.div(margin[0, d * per + t], jnp.int32(owned)) for t in range(per)]
     place = []
     for t in range(per):
@@ -329,7 +329,9 @@
 
 
 def mean_kernel(
-    owners, per, owned, slots, margin_h, arrived_h, out_h, margin, arrived, nothing, sums, load_sem, sems
+    owners, per, owned, slots,
+    margin_h, arrived_h, out_h,
+    margin, arrived, nothing, sums, down, right, load_sem, sems,
 ):
     d = lax.axis_index("visit")
     tile = nothing.shape[0]
@@ -357,6 +359,9 @@
         return carry
 
     lax.fori_loop(0, owned, zero, 0)
+    for i, j in enumerate(list(range(slots)) + list(range(2 * slots, 3 * slots))):
+        down[i] = one_hot(tile, margin[1, tiles[j]])
+        right[i] = one_hot(tile, -margin[2, tiles[j]])
     load.wait()
 
     for j in list(range(slots, 2 * slots)) + list(range(slots)) + list(range(2 * slots, 3 * slots)):
@@ -371,8 +376,8 @@
         def _():
             x = arrived[j]
             if not slots <= j < 2 * slots:
-                t = tiles[j]
-                x = moved(one_hot(tile, margin[1, t]), x, one_hot(tile, -margin[2, t]))
+                i = j if j < slots else j - slots
+                x = moved(down[i], x, right[i])
             count = jnp.full((1, 1), before + after + 1, jnp.int32).astype(F32)
             value = x.astype(F32) * (1.0 / count)
 
@@ -454,6 +459,8 @@
             pltpu.VMEM(arrived.shape, BF),
             pltpu.VMEM((tile, tile), F32),
             pltpu.VMEM(patches.shape, F32),
+            pltpu.VMEM((2 * slots, tile, tile), BF),
+            pltpu.VMEM((2 * slots, tile, tile), BF),
             dma((2,)),
             dma((owned,)),
         ],

time: 24.3 us -> 24.5 us (level); the launches traced: 24 us -> 24.5 us
  Pallas kernels: 24 us -> 24.5 us
    pallas_call x1, Pallas kernels: 3 us -> 3.55 us  [body(): pl.pallas_call(functools.partial(mean_kernel, owners, per, owned, slots),...]
where the time goes in v4:
time: 24.5 us
  Pallas kernels  24.5 us (100%)
    pallas_call x1, Pallas kernels, body(): pl.pallas_call(functools.partial(match_kernel, owners, per, owned, tile,...  21 us
    pallas_call x1, Pallas kernels, body(): pl.pallas_call(functools.partial(mean_kernel, owners, per, owned, slots),...  3.55 us

profile of v4, /device:TPU:1, one launch (start us, length us, event | category | flops | bytes accessed | tf_op | source)
XLA Modules:
  0.0 24.5 jit_solution(12146836492761124341)
XLA Ops:
  0.0 21.0 %match.1.arrived_h = bf16[6,256,256]{2,1,0:T(8,128)(2,1)} custom-call(s32[3,64]{1,0:T(4,128)} %bitcast.2, f32[4,27]{1,0:T(4,128)} %bitcast.4, s32[16]{0:T(128)} %ccd_h.1, f32[8,256,256]{2,1,0:T(8,128)} %patches_h.1, f32[256,1024]{1,0:T(8,128)} %science_h.1), custom_call_target="tpu_custom_call" | custom-call | tf_op jit(solution)/shard_map/match/pallas_call | solution.py:416
  21.0 3.6 %mean.1 = f32[8,256,256]{2,1,0:T(8,128)} custom-call(s32[3,64]{1,0:T(4,128)} %bitcast.3, bf16[6,256,256]{2,1,0:T(8,128)(2,1)} %match.1.arrived_h), custom_call_target="tpu_custom_call" | custom-call | tf_op jit(solution)/shard_map/mean/pallas_call | solution.py:452

commit v5 on v4

--- a/solution.py
+++ b/solution.py
@@ -71,7 +71,8 @@
     owners, per, owned, tile, slots,
     margin_h, coef_h, ccd_h, patches_h, science_h,
     out,
-    margin, coef, ccd, patches, science, stage, pool, ext, halo, tab, mixed, across, column, diff, parcel, back,
+    margin, coef, ccd, patches, science, stage, early, late, ext, halo_out, halo, tab, mixed, across, across_side,
+    column, side_column, matched, diff, parcel, back,
     load_sem, tile_send, tile_recv, halo_send, halo_recv, back_send, back_recv, out_sem,
 ):
     d = lax.axis_index("visit")
@@ -81,7 +82,6 @@
     chunk = tile // chunks
     depth = chunk + 2 * EDGE
     width = tile + SIDE
-    places = 3 * slots
 
     barrier = pltpu.get_barrier_semaphore()
 
@@ -94,15 +94,19 @@
         pl.semaphore_signal(barrier, inc=1, device_id={"visit": high}, device_id_type=pl.DeviceIdType.MESH)
 
     patch_load = pltpu.make_async_copy(patches_h, patches, load_sem.at[0])
-    science_load = pltpu.make_async_copy(science_h, science, load_sem.at[1])
+    science_loads = [
+        pltpu.make_async_copy(science_h.at[:, pl.ds(t * tile, tile)], science.at[t], load_sem.at[4 + t])
+        for t in range(per)
+    ]
     margin_load = pltpu.make_async_copy(margin_h, margin, load_sem.at[2])
-    coef_load = pltpu.make_async_copy(coef_h, coef, load_sem.at[3])
-    ccd_load = pltpu.make_async_copy(ccd_h, ccd, load_sem.at[4])
+    coef_load = pltpu.make_async_copy(coef_h, coef, load_sem.at[1])
+    ccd_load = pltpu.make_async_copy(ccd_h, ccd, load_sem.at[3])
     margin_load.start()
     patch_load.start()
     coef_load.start()
     ccd_load.start()
-    science_load.start()
+    for load in science_loads:
+        load.start()
     margin_load.wait()
 
     high_tiles, high_local, _ = named_tiles(margin, high, d, owners, per, owned, slots)
@@ -118,11 +122,13 @@
         )
 
     def tile_to_high(k, target):
-        return remote(stage.at[k], pool.at[k], tile_send.at[k], tile_recv.at[k], target)
+        dst = early.at[0] if k == 0 else late.at[k - 1]
+        return remote(stage.at[k], dst, tile_send.at[k], tile_recv.at[k], target)
 
     def tile_to_low(k, target):
         j = slots + k
-        return remote(stage.at[j], pool.at[2 * slots + k], tile_send.at[j], tile_recv.at[j], target)
+        dst = early.at[slots + 1] if k == 0 else late.at[slots + k - 2]
+        return remote(stage.at[j], dst, tile_send.at[j], tile_recv.at[j], target)
 
     def aligned(t, local):
         return moved(one_hot(tile, -margin[1, t]), patches[local].astype(BF), one_hot(tile, margin[2, t]))
@@ -138,11 +144,21 @@
         r = lax.broadcasted_iota(jnp.int32, (SIDE, tile), 0)
         c = lax.broadcasted_iota(jnp.int32, (SIDE, tile), 1)
         side = jnp.where(r < SIDE // 2, r + tile, r - SIDE)
-        w = (jnp.where(b * SIDE < tile, r + b * SIDE, side) - c).astype(F32)
+        main = b * SIDE < tile
+        w = (jnp.where(main, r + b * SIDE, side) - c).astype(F32)
         for g in range(SIGMAS):
             for h, table in enumerate(basis_functions(w, g)):
-                start = pl.multiple_of((g * ORDERS + h) * width + b * SIDE, SIDE)
-                across[pl.ds(start, SIDE), :] = table.astype(BF)
+                p = g * ORDERS + h
+                table = table.astype(BF)
+
+                @pl.when(main)
+                def _():
+                    across[pl.ds(pl.multiple_of(p * tile + b * SIDE, SIDE), SIDE), :] = table
+
+                @pl.when(jnp.logical_not(main))
+                def _():
+                    across_side[pl.ds(p * SIDE, SIDE), :] = table
+
         return carry
 
     lax.fori_loop(0, width // SIDE, across_rows, 0)
@@ -163,52 +179,94 @@
             tile_to_low(k, low).start()
 
     for k in range(slots):
-        pool[slots + k] = aligned(own_tiles[k], own_local[k])
+        early[1 + k] = aligned(own_tiles[k], own_local[k])
     coef_load.wait()
     ccd_load.wait()
 
-    def mix_tile(t, carry):
+    who = [lax.div(margin[0, d * per + t], jnp.int32(owned)) for t in range(per)]
+    ranks = [sum([(who[s] == who[t]).astype(jnp.int32) for s in range(t)], jnp.int32(0)) for t in range(per)]
+    keys = [jnp.where(who[t] == d, 0, 1 + ranks[t]) for t in range(per)]
+    position = []
+    for t in range(per):
+        ahead = [(keys[s] <= keys[t]) if s < t else (keys[s] < keys[t]) for s in range(per) if s != t]
+        position.append(sum([x.astype(jnp.int32) for x in ahead], jnp.int32(0)))
+
+    def at_position(values, q):
+        return sum([jnp.where(position[t] == q, values[t], 0) for t in range(per)], jnp.int32(0))
+
+    order = [at_position(list(range(per)), q) for q in range(per)]
+    is_late = [at_position([(keys[t] > 1).astype(jnp.int32) for t in range(per)], q) for q in range(per)]
+    side = [who[t] - d for t in range(per)]
+    early_place = [
+        jnp.where(side[t] == 0, 1 + ranks[t], jnp.where(side[t] < 0, 0, slots + 1)) for t in range(per)
+    ]
+    late_place = [jnp.maximum(ranks[t] - 1, 0) + jnp.where(side[t] < 0, 0, slots - 1) for t in range(per)]
+    early_at = [jnp.clip(at_position(early_place, q), 0, slots + 1) for q in range(per)]
+    late_at = [jnp.clip(at_position(late_place, q), 0, 2 * slots - 3) for q in range(per)]
+    right_at, left_at = [], []
+    for q in range(per):
+        right_at.append(sum([jnp.where(order[q] == t - 1, position[t], 0) for t in range(1, per)], jnp.int32(0)))
+        left_at.append(sum([jnp.where(order[q] == t + 1, position[t], 0) for t in range(per - 1)], jnp.int32(0)))
+
+    def mix_tile(q, carry):
+        t = order[0]
+        for i in range(1, per):
+            t = jnp.where(q == i, order[i], t)
         for g in range(SIGMAS):
             for h in range(ORDERS):
                 p = g * ORDERS + h
                 total = coef[t, p * ORDERS] * tab[g * ORDERS]
                 for v in range(1, ORDERS):
                     total = total + coef[t, p * ORDERS + v] * tab[g * ORDERS + v]
-                mixed[t, pl.ds(p * chunk, chunk), :] = total.astype(BF)
+                mixed[q, pl.ds(p * chunk, chunk), :] = total.astype(BF)
         return carry
 
     lax.fori_loop(0, per, mix_tile, 0)
 
-    who = [lax.div(margin[0, d * per + t], jnp.int32(owned)) for t in range(per)]
-    place = []
+    def tiles_arrive(k):
+        @pl.when(has_low)
+        def _():
+            tile_to_high(k, low).wait_recv()
+
+        @pl.when(has_high)
+        def _():
+            tile_to_low(k, high).wait_recv()
+
+    def down_columns(q, c, at):
+        window = pl.ds(pl.multiple_of(c * chunk, chunk), depth)
+        result = jnp.dot(mixed[q], ext[q, window, pl.ds(0, tile)], preferred_element_type=F32).astype(BF)
+        for p in range(PAIRS):
+            column[pl.ds(at * chunk, chunk), pl.ds(p * tile, tile)] = result[p * chunk : (p + 1) * chunk]
+
+    half = per // 2
+    tiles_arrive(0)
+
+    def middle(first):
+        for q in range(half):
+            for i in range(2):
+                down_columns(first + q, 1 + i, 2 * q + i)
+        result = jnp.dot(column[...], across[...], preferred_element_type=F32)
+        for q in range(half):
+            matched[first + q, pl.ds(chunk, 2 * chunk), :] = result[2 * q * chunk : 2 * (q + 1) * chunk]
+
+    for q in range(half):
+        ext[q, pl.ds(EDGE, tile), pl.ds(0, tile)] = early[early_at[q]]
+    middle(0)
+    for k in range(1, slots):
+        tiles_arrive(k)
+    for q in range(half, per):
+        x = jnp.where(is_late[q] == 1, late[late_at[q]].astype(F32), early[early_at[q]].astype(F32)).astype(BF)
+        ext[q, pl.ds(EDGE, tile), pl.ds(0, tile)] = x
+
+    def halo_to_high(target):
+        return remote(halo_out.at[0], halo.at[0], halo_send.at[0], halo_recv.at[0], target)
+
+    def halo_to_low(target):
+        return remote(halo_out.at[1], halo.at[1], halo_send.at[1], halo_recv.at[1], target)
+
     for t in range(per):
-        rank = jnp.int32(0)
-        for s in range(t):
-            rank = rank + (who[s] == who[t]).astype(jnp.int32)
-        place.append(jnp.clip((who[t] - d + 1) * slots + rank, 0, places - 1))
-
-    for k in range(slots):
-
-        @pl.when(has_low)
-        def _():
-            tile_to_high(k, low).wait_recv()
-
-        @pl.when(has_high)
-        def _():
-            tile_to_low(k, high).wait_recv()
-
-    for t in range(per):
-        ext[t, pl.ds(EDGE, tile), pl.ds(0, tile)] = pool[place[t]]
-
-    def halo_to_high(target):
-        return remote(
-            ext.at[:, pl.ds(tile, EDGE), pl.ds(0, tile)], halo.at[0], halo_send.at[0], halo_recv.at[0], target
-        )
-
-    def halo_to_low(target):
-        return remote(
-            ext.at[:, pl.ds(EDGE, EDGE), pl.ds(0, tile)], halo.at[1], halo_send.at[1], halo_recv.at[1], target
-        )
+        halo_out[0, t] = ext[position[t], pl.ds(tile, EDGE), pl.ds(0, tile)]
+        halo_out[1, t] = ext[position[t], pl.ds(EDGE, EDGE), pl.ds(0, tile)]
 
     @pl.when(has_high)
     def _():
@@ -221,13 +279,17 @@
     def fill_sides(first, count):
         lane = lax.broadcasted_iota(jnp.int32, (count, SIDE), 1)
         none = jnp.zeros((count, SIDE), F32)
-        for t in range(per):
-            right = ext[t + 1, pl.ds(first, count), pl.ds(0, SIDE)].astype(F32) if t + 1 < per else none
-            left = ext[t - 1, pl.ds(first, count), pl.ds(tile - SIDE, SIDE)].astype(F32) if t > 0 else none
-            ext[t, pl.ds(first, count), pl.ds(tile, SIDE)] = jnp.where(lane < SIDE // 2, right, left).astype(BF)
+        for q in range(per):
+            right = ext[right_at[q], pl.ds(first, count), pl.ds(0, SIDE)].astype(F32)
+            left = ext[left_at[q], pl.ds(first, count), pl.ds(tile - SIDE, SIDE)].astype(F32)
+            right = jnp.where(order[q] + 1 < per, right, none)
+            left = jnp.where(order[q] > 0, left, none)
+            ext[q, pl.ds(first, count), pl.ds(tile, SIDE)] = jnp.where(lane < SIDE // 2, right, left).astype(BF)
 
     fill_sides(EDGE, tile)
-    science_load.wait()
+    middle(half)
+    for load in science_loads:
+        load.wait()
 
     def chunk_to_low(k, c, target):
         at = pl.ds(pl.multiple_of(c * chunk, chunk), chunk)
@@ -240,6 +302,9 @@
         at = pl.ds(pl.multiple_of(c * chunk, chunk), chunk)
         return remote(parcel.at[j, at], out.at[k, at], back_send.at[c, j], back_recv.at[c, j], target)
 
+    def position_of(t):
+        return sum([jnp.where(t - d * per == s, position[s], 0) for s in range(per)], jnp.int32(0))
+
     def one_chunk(i, carry):
         c = lax.rem(i + 1, chunks)
         at = pl.ds(pl.multiple_of(c * chunk, chunk), chunk)
@@ -258,23 +323,35 @@
             keep_bottom = has_high & (ccd[jnp.minimum(d + 1, owners - 1)] == 0)
             nothing = jnp.zeros((EDGE, tile), BF)
             for t in range(per):
-                ext[t, pl.ds(0, EDGE), pl.ds(0, tile)] = jnp.where(keep_top, halo[0, t], nothing)
-                ext[t, pl.ds(EDGE + tile, EDGE), pl.ds(0, tile)] = jnp.where(keep_bottom, halo[1, t], nothing)
+                top = jnp.where(keep_top, halo[0, order[t]], nothing)
+                bottom = jnp.where(keep_bottom, halo[1, order[t]], nothing)
+                ext[t, pl.ds(0, EDGE), pl.ds(0, tile)] = top
+                ext[t, pl.ds(EDGE + tile, EDGE), pl.ds(0, tile)] = bottom
             fill_sides(0, EDGE)
             fill_sides(EDGE + tile, EDGE)
 
+        @pl.when(i >= chunks - 2)
+        def _():
+            for q in range(per):
+                down_columns(q, c, q)
+            result = jnp.dot(column[...], across[...], preferred_element_type=F32)
+            for q in range(per):
+                matched[q, at, :] = result[q * chunk : (q + 1) * chunk]
+
         window = pl.ds(pl.multiple_of(c * chunk, chunk), depth)
-        for t in range(per):
-            result = jnp.dot(mixed[t], ext[t, window, :], preferred_element_type=F32).astype(BF)
+        for q in range(per):
+            result = jnp.dot(
+                mixed[q], ext[q, window, pl.ds(tile, SIDE)], preferred_element_type=F32
+            ).astype(BF)
             for p in range(PAIRS):
-                column[pl.ds(t * chunk, chunk), pl.ds(p * width, width)] = result[p * chunk : (p + 1) * chunk]
-        matched = jnp.dot(column[...], across[...], preferred_element_type=F32)
-        for t in range(per):
-            sky = science[at, pl.ds(t * tile, tile)]
-            diff[t, at, :] = (sky - matched[t * chunk : (t + 1) * chunk]).astype(BF)
+                side_column[pl.ds(q * chunk, chunk), pl.ds(p * SIDE, SIDE)] = result[p * chunk : (p + 1) * chunk]
+        sides = jnp.dot(side_column[...], across_side[...], preferred_element_type=F32)
+        for q in range(per):
+            sky = science[order[q], at, :]
+            diff[q, at, :] = (sky - (matched[q, at, :] + sides[q * chunk : (q + 1) * chunk])).astype(BF)
         for k in range(slots):
-            parcel[k, at, :] = diff[from_low[k] - d * per, at, :]
-            parcel[slots + k, at, :] = diff[from_high[k] - d * per, at, :]
+            parcel[k, at, :] = diff[position_of(from_low[k]), at, :]
+            parcel[slots + k, at, :] = diff[position_of(from_high[k]), at, :]
 
             @pl.when(has_low)
             def _():
@@ -293,7 +370,7 @@
 
     for k in range(slots):
         t = own_tiles[k]
-        back[k] = moved(one_hot(tile, margin[1, t]), diff[t - d * per], one_hot(tile, -margin[2, t]))
+        back[k] = moved(one_hot(tile, margin[1, t]), diff[position_of(t)], one_hot(tile, -margin[2, t]))
         own_copy(k).start()
 
     @pl.when(has_low)
@@ -423,19 +500,24 @@
             pltpu.SMEM(kernel_coef.shape[::-1], F32),
             pltpu.SMEM(ccd_first.shape, jnp.int32),
             pltpu.VMEM((owned, tile, tile), F32),
-            pltpu.VMEM((tile, per * tile), F32),
+            pltpu.VMEM((per, tile, tile), F32),
             pltpu.VMEM((2 * slots, tile, tile), BF),
-            pltpu.VMEM((3 * slots, tile, tile), BF),
+            pltpu.VMEM((slots + 2, tile, tile), BF),
+            pltpu.VMEM((2 * slots - 2, tile, tile), BF),
             pltpu.VMEM((per, tile + 2 * EDGE, width), BF),
+            pltpu.VMEM((2, per, EDGE, tile), BF),
             pltpu.VMEM((2, per, EDGE, tile), BF),
             pltpu.VMEM((PAIRS, chunk, depth), F32),
             pltpu.VMEM((per, PAIRS * chunk, depth), BF),
-            pltpu.VMEM((PAIRS * width, tile), BF),
-            pltpu.VMEM((per * chunk, PAIRS * width), BF),
+            pltpu.VMEM((PAIRS * tile, tile), BF),
+            pltpu.VMEM((PAIRS * SIDE, tile), BF),
+            pltpu.VMEM((per * chunk, PAIRS * tile), BF),
+            pltpu.VMEM((per * chunk, PAIRS * SIDE), BF),
+            pltpu.VMEM((per, tile, tile), F32),
             pltpu.VMEM((per, tile, tile), BF),
             pltpu.VMEM((2 * slots, tile, tile), BF),
             pltpu.VMEM((slots, tile, tile), BF),
-            dma((5,)),
+            dma((4 + per,)),
             dma((2 * slots,)),
             dma((2 * slots,)),
             dma((2,)),

time: 24.5 us -> 23.9 us (0.976); the launches traced: 24.5 us -> 23.6 us
  Pallas kernels: 24.5 us -> 23.6 us
    pallas_call x1, Pallas kernels: 3.55 us -> 2.8 us  [body(): pl.pallas_call(functools.partial(mean_kernel, owners, per, owned, slots),...]
where the time goes in v5:
time: 23.9 us; the launch traced here: 23.6 us
  Pallas kernels  23.6 us (99%)
    pallas_call x1, Pallas kernels, body(): pl.pallas_call(functools.partial(match_kernel, owners, per, owned, tile,...  20.8 us
    pallas_call x1, Pallas kernels, body(): pl.pallas_call(functools.partial(mean_kernel, owners, per, owned, slots),...  2.8 us

profile of v5, /device:TPU:1, one launch (start us, length us, event | category | flops | bytes accessed | tf_op | source)
XLA Modules:
  0.0 23.6 jit_solution(13484046878469451007)
XLA Ops:
  0.0 20.8 %match.1.arrived_h = bf16[6,256,256]{2,1,0:T(8,128)(2,1)} custom-call(s32[3,64]{1,0:T(4,128)} %bitcast.2, f32[4,27]{1,0:T(4,128)} %bitcast.4, s32[16]{0:T(128)} %ccd_h.1, f32[8,256,256]{2,1,0:T(8,128)} %patches_h.1, f32[256,1024]{1,0:T(8,128)} %science_h.1), custom_call_target="tpu_custom_call" | custom-call | tf_op jit(solution)/shard_map/match/pallas_call | solution.py:493
  20.8 2.8 %mean.1 = f32[8,256,256]{2,1,0:T(8,128)} custom-call(s32[3,64]{1,0:T(4,128)} %bitcast.3, bf16[6,256,256]{2,1,0:T(8,128)(2,1)} %match.1.arrived_h), custom_call_target="tpu_custom_call" | custom-call | tf_op jit(solution)/shard_map/mean/pallas_call | solution.py:534
